TPU v7x, 32 devices: a whole 2x2x4 slice. The times are simulated.
32 devices in a mesh: pipe: 4 (over y, core), tensor: 8 (over z, x).
Axes of the slice: x: 2, y: 2, z: 4, core: 2. Of those that a mesh axis runs over, the one named last changes fastest.
Arguments:
- inputs: bfloat16 [128, 4096], P(None, 'tensor'), may hold values from -6 to 6
- out_grad: bfloat16 [128, 4096], P(None, 'tensor'), may hold values from -6 to 6
- norm_gain: float32 [4, 4096], P('pipe'), may hold values from 0.25 to 1.75
- gate_weight: bfloat16 [4, 4096, 14336], P('pipe', None, 'tensor'), may hold values from -0.125 to 0.125
- up_weight: bfloat16 [4, 4096, 14336], P('pipe', None, 'tensor'), may hold values from -0.125 to 0.125
- down_weight: bfloat16 [4, 14336, 4096], P('pipe', 'tensor'), may hold values from -0.0625 to 0.0625
- block_mask: int32 [4, 3, 32, 112], P('pipe', None, None, 'tensor'), may hold values from 0 to 1, as said below
Outputs:
- section_out: float32 [4, 128, 4096], P('pipe')
- section_grad: float32 [4, 128, 4096], P('pipe')
Inputs may be any that keep to these rules, and one draw needn't show every extreme that they name: `block_mask`: 1 keeps a block, 0 drops it; the share kept differs from one block column to another.
All inputs are finite; a program needn't handle non-finite values.
Results may differ from a plain program's by a relative error of at most 0.02.
Values may be sent and summed in bfloat16 or wider, within the bound.
No kernel may reach another device: no remote copies, remote signals or barrier semaphores. Data moves between devices by JAX's collectives and lax.ppermute only.
A program may use at most 192 MiB of HBM per device.

v0:
```python
import jax
import jax.numpy as jnp
from jax import lax
from jax.sharding import PartitionSpec as P

BLOCK = 128
ROWS = 64


def shifted(value, axis, steps):
    count = lax.axis_size(axis)
    first, last = (max(0, -steps), min(count, count - steps))
    return lax.ppermute(value, axis, [(source, source + steps) for source in range(first, last)])


def masked_blocks(weight, mask):
    rows, cols = weight.shape
    shaped = weight.reshape(rows // BLOCK, BLOCK, cols // BLOCK, BLOCK)
    return (shaped * mask.astype(weight.dtype)[:, None, :, None]).reshape(rows, cols)


def contract_last(left, right):
    return lax.dot_general(
        left, right, (((1,), (1,)), ((), ())), preferred_element_type=jnp.float32
    )


def norm_back(xval, avec, scale):
    inner = jnp.mean(avec * xval, axis=-1, keepdims=True)
    return scale * avec - xval * scale * scale * scale * inner


def retain_place(buffer, value, store_place, valid_flag):
    older = lax.dynamic_index_in_dim(buffer, store_place, 0, keepdims=False)
    return lax.dynamic_update_index_in_dim(
        buffer, jnp.where(valid_flag, value, older), store_place, 0
    )


def local(inputs, out_grad, norm_gain, gate_weight, up_weight, down_weight, block_mask):
    eps = 1e-05
    whole_in, whole_grad = (
        lax.all_gather(inputs, "tensor", axis=1, tiled=True),
        lax.all_gather(out_grad, "tensor", axis=1, tiled=True),
    )
    width = whole_in.shape[1]
    count = whole_in.shape[0] // ROWS
    whole_in = whole_in.reshape(count, ROWS, width)
    whole_grad = whole_grad.reshape(count, ROWS, width)
    gmat = masked_blocks(gate_weight[0], block_mask[0, 0])
    umat = masked_blocks(up_weight[0], block_mask[0, 1])
    dmat = masked_blocks(down_weight[0], block_mask[0, 2].T)
    gain = norm_gain[0]
    hidden_cols = gmat.shape[1]
    section = lax.axis_index("pipe")
    sections = lax.axis_size("pipe")
    step_total = count + sections - 1
    sent_rows = ROWS

    def forward_step_once(tick, loop_state):
        arriving_rows, input_store, gate_store, upper_store, output_store = loop_state
        micro = tick - section
        valid_flag = (micro >= 0) & (micro < count)
        store_place = jnp.clip(micro, 0, count - 1)
        first = lax.dynamic_index_in_dim(whole_in, store_place, 0, keepdims=False).astype(
            jnp.float32
        )
        xval = jnp.where(section == 0, first, arriving_rows)
        scale = lax.rsqrt(jnp.mean(xval * xval, axis=-1, keepdims=True) + eps)
        normed = (xval * scale * gain).astype(jnp.bfloat16)
        gate_matrix = jnp.dot(normed, gmat, preferred_element_type=jnp.float32)
        upval = jnp.dot(normed, umat, preferred_element_type=jnp.float32)
        hidden = (jax.nn.silu(gate_matrix) * upval).astype(jnp.bfloat16)
        partial_out = jnp.dot(hidden, dmat, preferred_element_type=jnp.float32)
        summed = lax.psum(partial_out, "tensor")
        result = xval + summed
        input_store = retain_place(input_store, xval, store_place, valid_flag)
        gate_store = retain_place(gate_store, gate_matrix, store_place, valid_flag)
        upper_store = retain_place(upper_store, upval, store_place, valid_flag)
        output_store = retain_place(output_store, result, store_place, valid_flag)
        handed_rows = shifted(result, "pipe", 1)
        return (handed_rows, input_store, gate_store, upper_store, output_store)

    first_position = (
        jnp.zeros((sent_rows, width), jnp.float32),
        jnp.zeros((count, ROWS, width), jnp.float32),
        jnp.zeros((count, ROWS, hidden_cols), jnp.float32),
        jnp.zeros((count, ROWS, hidden_cols), jnp.float32),
        jnp.zeros((count, sent_rows, width), jnp.float32),
    )
    unused_value, input_store, gate_store, upper_store, output_store = lax.fori_loop(
        0, step_total, forward_step_once, first_position
    )

    def backward_tick(tick, loop_state):
        arriving_rows, dbuf = loop_state
        micro = tick - (sections - 1 - section)
        valid_flag = (micro >= 0) & (micro < count)
        store_place = jnp.clip(micro, 0, count - 1)
        last = lax.dynamic_index_in_dim(whole_grad, store_place, 0, keepdims=False).astype(
            jnp.float32
        )
        cot = jnp.where(section == sections - 1, last, arriving_rows)
        xval = lax.dynamic_index_in_dim(input_store, store_place, 0, keepdims=False)
        gate_matrix = lax.dynamic_index_in_dim(gate_store, store_place, 0, keepdims=False)
        upval = lax.dynamic_index_in_dim(upper_store, store_place, 0, keepdims=False)
        dhid = contract_last(cot.astype(jnp.bfloat16), dmat)
        sig = jax.nn.sigmoid(gate_matrix)
        dgate = (dhid * upval * sig * (1.0 + gate_matrix * (1.0 - sig))).astype(jnp.bfloat16)
        dup = (dhid * gate_matrix * sig).astype(jnp.bfloat16)
        partial_grad = contract_last(dgate, gmat) + contract_last(dup, umat)
        dnorm = lax.psum(partial_grad, "tensor")
        scale = lax.rsqrt(jnp.mean(xval * xval, axis=-1, keepdims=True) + eps)
        result = cot + norm_back(xval, dnorm * gain, scale)
        dbuf = retain_place(dbuf, result, store_place, valid_flag)
        handed_rows = shifted(result, "pipe", -1)
        return (handed_rows, dbuf)

    begin = (
        jnp.zeros((sent_rows, width), jnp.float32),
        jnp.zeros((count, sent_rows, width), jnp.float32),
    )
    unused_value, dbuf = lax.fori_loop(0, step_total, backward_tick, begin)
    return (output_store.reshape(1, count * ROWS, width), dbuf.reshape(1, count * ROWS, width))


def solution(mesh):
    in_specs = (
        P(None, "tensor"),
        P(None, "tensor"),
        P("pipe", None),
        P("pipe", None, "tensor"),
        P("pipe", None, "tensor"),
        P("pipe", "tensor", None),
        P("pipe", None, None, "tensor"),
    )
    out_specs = (P("pipe", None, None), P("pipe", None, None))
    return jax.shard_map(local, mesh=mesh, in_specs=in_specs, out_specs=out_specs, check_vma=False)
```

profile of v0, /device:TPU:0, one launch (start us, length us, event | category | flops | bytes accessed | tf_op | source)
XLA Modules:
  0.0 1463.0 jit_solution(18320694511615378771)
XLA Ops:
  8.7 19.7 %copy.12 = bf16[1,4096,1792]{1,2,0:T(8,128)(2,1)} copy(bf16[1,4096,1792]{2,1,0:T(8,128)(2,1)} %param.15) | data formatting | bytes 29360128 | tf_op args[4]
  35.5 19.3 %bitcast_multiply_fusion.7 = bf16[4096,1792]{0,1:T(8,128)(2,1)} fusion(bf16[224,8,32,128]{3,2,1,0:T(8,128)(2,1)} %bitcast.202, bf16[1,4096,1792]{1,2,0:T(8,128)(2,1)} %copy.12), kind=kLoop, calls=%fused_computation.65 | loop fusion | flops 7340032 | bytes 44040192 | tf_op jit(solution)/shard_map/mul | solution.py:19
  54.8 18.8 %copy.14 = bf16[4096,1792]{1,0:T(8,128)(2,1)} copy(bf16[4096,1792]{0,1:T(8,128)(2,1)} %bitcast_multiply_fusion.7) | data formatting | bytes 29360128 | tf_op jit(solution)/shard_map/while | solution.py:91
  73.6 20.2 %copy.11 = bf16[1,4096,1792]{1,2,0:T(8,128)(2,1)} copy(bf16[1,4096,1792]{2,1,0:T(8,128)(2,1)} %param.14) | data formatting | bytes 29360128 | tf_op args[3]
  100.8 19.2 %bitcast_multiply_fusion.8 = bf16[4096,1792]{0,1:T(8,128)(2,1)} fusion(bf16[224,8,32,128]{3,2,1,0:T(8,128)(2,1)} %bitcast.203, bf16[1,4096,1792]{1,2,0:T(8,128)(2,1)} %copy.11), kind=kLoop, calls=%fused_computation.66 | loop fusion | flops 7340032 | bytes 44040192 | tf_op jit(solution)/shard_map/mul | solution.py:19
  120.1 18.7 %copy.13 = bf16[4096,1792]{1,0:T(8,128)(2,1)} copy(bf16[4096,1792]{0,1:T(8,128)(2,1)} %bitcast_multiply_fusion.8) | data formatting | bytes 29360128 | tf_op jit(solution)/shard_map/while | solution.py:91
  145.9 19.3 %bitcast_multiply_fusion.6 = bf16[1792,4096]{1,0:T(8,128)(2,1)} fusion(bf16[224,8,32,128]{3,2,1,0:T(8,128)(2,1)} %bitcast.204, bf16[1,1792,4096]{2,1,0:T(8,128)(2,1)} %param.16), kind=kLoop, calls=%fused_computation.64 | loop fusion | flops 7340032 | bytes 44040192 | tf_op jit(solution)/shard_map/mul | solution.py:19
  170.3 599.5 %while.39 = (s32[]{:T(128)}, f32[64,4096]{1,0:T(8,128)S(1)}, f32[2,64,4096]{2,1,0:T(8,128)}, f32[2,64,1792]{2,1,0:T(8,128)}, f32[2,64,1792]{2,1,0:T(8,128)}, /*i...) while((s32[]{:T(128)}, f32[64,4096]{1,0:T(8,128)S(1)}, ...), condition=%wide.region_3.4_spmd, body=%wide.region_0.3_spmd.sunk | while | flops 2823421952 | bytes 194005200 | solution.py:91
  196.9 78.4 %all-reduce.3.cloned.1.call-done = f32[64,4096]{1,0:T(8,128)} async-done(((f32[64,4096]{1,0:T(8,128)}), f32[64,4096]{1,0:T(8,128)}) %all-reduce.3.cloned.1.call-update) | async-done | bytes 1048592 | tf_op jit(solution)/shard_map/while/body/eval_jaxpr/psum | solution.py:75
  309.3 87.7 %all-reduce.3.cloned.1.call-done = f32[64,4096]{1,0:T(8,128)} async-done(((f32[64,4096]{1,0:T(8,128)}), f32[64,4096]{1,0:T(8,128)}) %all-reduce.3.cloned.1.call-update) | async-done | bytes 1048592 | tf_op jit(solution)/shard_map/while/body/eval_jaxpr/psum | solution.py:75
  431.0 87.8 %all-reduce.3.cloned.1.call-done = f32[64,4096]{1,0:T(8,128)} async-done(((f32[64,4096]{1,0:T(8,128)}), f32[64,4096]{1,0:T(8,128)}) %all-reduce.3.cloned.1.call-update) | async-done | bytes 1048592 | tf_op jit(solution)/shard_map/while/body/eval_jaxpr/psum | solution.py:75
  552.8 87.7 %all-reduce.3.cloned.1.call-done = f32[64,4096]{1,0:T(8,128)} async-done(((f32[64,4096]{1,0:T(8,128)}), f32[64,4096]{1,0:T(8,128)}) %all-reduce.3.cloned.1.call-update) | async-done | bytes 1048592 | tf_op jit(solution)/shard_map/while/body/eval_jaxpr/psum | solution.py:75
  674.5 87.8 %all-reduce.3.cloned.1.call-done = f32[64,4096]{1,0:T(8,128)} async-done(((f32[64,4096]{1,0:T(8,128)}), f32[64,4096]{1,0:T(8,128)}) %all-reduce.3.cloned.1.call-update) | async-done | bytes 1048592 | tf_op jit(solution)/shard_map/while/body/eval_jaxpr/psum | solution.py:75
  770.5 53.8 %all-gather.5.cloned.1.call-done = bf16[128,4096]{1,0:T(8,128)(2,1)} async-done(((bf16[128,512]{1,0:T(8,128)(2,1)}), bf16[128,4096]{1,0:T(8,128)(2,1)}) %all-gather.5.cloned.1.call-update) | async-done | bytes 1048592 | tf_op jit(solution)/shard_map/all_gather | solution.py:44
  826.0 630.2 %while.40 = (s32[]{:T(128)}, f32[64,4096]{1,0:T(8,128)S(1)}, f32[2,64,4096]{2,1,0:T(8,128)}, pred[]{:T(512)}, s32[]{:T(128)}, /*index=5*/bf16[2,64,4096]{2,1,0:T...) while((s32[]{:T(128)}, f32[64,4096]{1,0:T(8,128)S(1)}, ...), condition=%wide.region_8.9_spmd, body=%wide.region_4.8_spmd.sunk | while | flops 2825650432 | bytes 92442024 | solution.py:123
  846.1 10.8 convolution_add_fusion.2
  859.2 74.8 %all-reduce.5.cloned.1.call-done = f32[64,4096]{1,0:T(8,128)} async-done(((f32[64,4096]{1,0:T(8,128)}), f32[64,4096]{1,0:T(8,128)}) %all-reduce.5.cloned.1.call-update) | async-done | bytes 1048592 | tf_op jit(solution)/shard_map/while/body/eval_jaxpr/psum | solution.py:112
  963.4 10.8 convolution_add_fusion.2
  976.5 85.5 %all-reduce.5.cloned.1.call-done = f32[64,4096]{1,0:T(8,128)} async-done(((f32[64,4096]{1,0:T(8,128)}), f32[64,4096]{1,0:T(8,128)}) %all-reduce.5.cloned.1.call-update) | async-done | bytes 1048592 | tf_op jit(solution)/shard_map/while/body/eval_jaxpr/psum | solution.py:112
  1091.6 10.8 convolution_add_fusion.2
  1104.7 85.5 %all-reduce.5.cloned.1.call-done = f32[64,4096]{1,0:T(8,128)} async-done(((f32[64,4096]{1,0:T(8,128)}), f32[64,4096]{1,0:T(8,128)}) %all-reduce.5.cloned.1.call-update) | async-done | bytes 1048592 | tf_op jit(solution)/shard_map/while/body/eval_jaxpr/psum | solution.py:112
  1232.8 85.5 %all-reduce.5.cloned.1.call-done = f32[64,4096]{1,0:T(8,128)} async-done(((f32[64,4096]{1,0:T(8,128)}), f32[64,4096]{1,0:T(8,128)}) %all-reduce.5.cloned.1.call-update) | async-done | bytes 1048592 | tf_op jit(solution)/shard_map/while/body/eval_jaxpr/psum | solution.py:112
  1347.8 10.8 convolution_add_fusion.2
  1360.9 85.5 %all-reduce.5.cloned.1.call-done = f32[64,4096]{1,0:T(8,128)} async-done(((f32[64,4096]{1,0:T(8,128)}), f32[64,4096]{1,0:T(8,128)}) %all-reduce.5.cloned.1.call-update) | async-done | bytes 1048592 | tf_op jit(solution)/shard_map/while/body/eval_jaxpr/psum | solution.py:112
  (327 shorter events, 369.2 us)
Async XLA Ops:
  7.2 158.0 %all-gather.3.cloned.1.call-start = ((), (), s32[]{:S(2)}) async-start(), calls=%async_computation | async-start | bytes 1179648 | tf_op jit(solution)/shard_map/all_gather | solution.py:43
  170.3 104.9 %all-reduce.3.cloned.1.call-start = ((), (), s32[]{:S(2)}) async-start(), calls=%async_computation.2 | async-start | bytes 2097152 | tf_op jit(solution)/shard_map/while/body/eval_jaxpr/psum | solution.py:75
  279.0 3.8 collective-permute-start
  282.8 114.2 %all-reduce.3.cloned.1.call-start = ((), (), s32[]{:S(2)}) async-start(), calls=%async_computation.2 | async-start | bytes 2097152 | tf_op jit(solution)/shard_map/while/body/eval_jaxpr/psum | solution.py:75
  400.7 3.8 collective-permute-start
  404.5 114.3 %all-reduce.3.cloned.1.call-start = ((), (), s32[]{:S(2)}) async-start(), calls=%async_computation.2 | async-start | bytes 2097152 | tf_op jit(solution)/shard_map/while/body/eval_jaxpr/psum | solution.py:75
  522.5 3.8 collective-permute-start
  526.3 114.2 %all-reduce.3.cloned.1.call-start = ((), (), s32[]{:S(2)}) async-start(), calls=%async_computation.2 | async-start | bytes 2097152 | tf_op jit(solution)/shard_map/while/body/eval_jaxpr/psum | solution.py:75
  644.2 3.8 collective-permute-start
  648.0 114.3 %all-reduce.3.cloned.1.call-start = ((), (), s32[]{:S(2)}) async-start(), calls=%async_computation.2 | async-start | bytes 2097152 | tf_op jit(solution)/shard_map/while/body/eval_jaxpr/psum | solution.py:75
  766.0 3.8 collective-permute-start
  769.8 54.6 %all-gather.5.cloned.1.call-start = ((), (), s32[]{:S(2)}) async-start(), calls=%async_computation.1 | async-start | bytes 1179648 | tf_op jit(solution)/shard_map/all_gather | solution.py:44
  826.2 107.7 %all-reduce.5.cloned.1.call-start = ((), (), s32[]{:S(2)}) async-start(), calls=%async_computation.3 | async-start | bytes 2097152 | tf_op jit(solution)/shard_map/while/body/eval_jaxpr/psum | solution.py:112
  938.9 4.8 collective-permute-start.1
  943.7 118.4 %all-reduce.5.cloned.1.call-start = ((), (), s32[]{:S(2)}) async-start(), calls=%async_computation.3 | async-start | bytes 2097152 | tf_op jit(solution)/shard_map/while/body/eval_jaxpr/psum | solution.py:112
  963.4 98.7 %copy-start.3 = (f32[2,64,4096]{2,1,0:T(8,128)S(1)}, f32[2,64,4096]{2,1,0:T(8,128)}, u32[]{:S(2)}) copy-start(f32[2,64,4096]{2,1,0:T(8,128)} %get-tuple-element.920) | copy-start | bytes 6291460 | tf_op jit(solution)/shard_map/while
  1067.0 4.8 collective-permute-start.1
  1071.8 118.4 %all-reduce.5.cloned.1.call-start = ((), (), s32[]{:S(2)}) async-start(), calls=%async_computation.3 | async-start | bytes 2097152 | tf_op jit(solution)/shard_map/while/body/eval_jaxpr/psum | solution.py:112
  1091.5 98.7 %copy-start.3 = (f32[2,64,4096]{2,1,0:T(8,128)S(1)}, f32[2,64,4096]{2,1,0:T(8,128)}, u32[]{:S(2)}) copy-start(f32[2,64,4096]{2,1,0:T(8,128)} %get-tuple-element.920) | copy-start | bytes 6291460 | tf_op jit(solution)/shard_map/while
  1195.1 4.8 collective-permute-start.1
  1199.9 118.4 %all-reduce.5.cloned.1.call-start = ((), (), s32[]{:S(2)}) async-start(), calls=%async_computation.3 | async-start | bytes 2097152 | tf_op jit(solution)/shard_map/while/body/eval_jaxpr/psum | solution.py:112
  1323.3 4.8 collective-permute-start.1
  1328.0 118.4 %all-reduce.5.cloned.1.call-start = ((), (), s32[]{:S(2)}) async-start(), calls=%async_computation.3 | async-start | bytes 2097152 | tf_op jit(solution)/shard_map/while/body/eval_jaxpr/psum | solution.py:112
  1451.4 4.8 collective-permute-start.1
  (89 other events, 1080.2 us)
Sparse Core Ops, SparseCore 0:
  10.0 42.2 all-gather.2
  194.3 80.9 all-reduce.2
  306.7 90.1 all-reduce.2
  428.4 90.2 all-reduce.2
  550.2 90.1 all-reduce.2
  671.9 90.2 all-reduce.2
  772.7 51.6 all-gather.4
  857.0 76.8 all-reduce.4
  974.4 87.6 all-reduce.4
  1102.5 87.6 all-reduce.4
  1230.6 87.6 all-reduce.4
  1358.8 87.6 all-reduce.4
where the time goes:
time: 1480 us; the launch traced here: 1460 us
  waiting for transfers between devices  931 us (63%)
  matrix products  229 us (15%)
  local copies, waits for them, and re-layouts  156 us (11%)
  other arithmetic  119 us (8%)
    psum x5, waiting for transfers between devices, forward_step_once(): summed = lax.psum(partial_out, 'tensor')  429 us
    psum x5, waiting for transfers between devices, backward_tick(): dnorm = lax.psum(partial_grad, 'tensor')  417 us
    dot_general x15, matrix products, contract_last(): lax.dot_general(left, right, (((1,), (1,)), ((), ())), preferred_element_...  153 us
    mul x3, other arithmetic, masked_blocks(): shaped * mask.astype(weight.dtype)[:, None, :, None]  57.8 us
    all_gather x1, waiting for transfers between devices, local(): lax.all_gather(out_grad, 'tensor', axis=1, tiled=True)  53.8 us
    dot_general x5, matrix products, forward_step_once(): upval = jnp.dot(normed, umat, preferred_element_type=jnp.float32)  44.6 us
    unnamed x5, local copies, waits for them, and re-layouts  39.8 us
    while x2, local copies, waits for them, and re-layouts, local(): lax.fori_loop(0, step_total, forward_step_once, first_position)  37.5 us
  transfers between devices with their start and end apart: 22, of which 21 were waited for; matrix products, arithmetic and copies ran while one was open for 12% of the time, Pallas kernels for 0%

commit v1 on v0

v1 whole, which is shorter than its diff:
```python
import functools

import jax
import jax.numpy as jnp
from jax import lax
from jax.experimental import pallas as pl
from jax.experimental.pallas import tpu as pltpu
from jax.sharding import PartitionSpec as P

BLOCK = 128
EPS = 1e-05
F32 = jnp.float32
BF16 = jnp.bfloat16
VMEM_WHOLE = pl.BlockSpec(memory_space=pltpu.VMEM)
SMEM_WHOLE = pl.BlockSpec(memory_space=pltpu.SMEM)
HBM_WHOLE = pl.BlockSpec(memory_space=pltpu.HBM)


def tile_of(size):
    return next(tile for tile in (256, 128) if size % tile == 0)


def contract_last(left, right):
    return lax.dot_general(left, right, (((1,), (1,)), ((), ())), preferred_element_type=F32)


def load_kernel(mask, gate_hbm, up_hbm, down_hbm, gate_out, up_out, down_out, sems):
    width, cols = gate_out.shape
    parts = sems.shape[1]
    wide_rows, deep_rows = width // parts, cols // parts

    def bring(which, part):
        source, target = ((gate_hbm, gate_out), (up_hbm, up_out), (down_hbm, down_out))[which]
        size = deep_rows if which == 2 else wide_rows
        here = pl.ds(part * size, size)
        return pltpu.make_async_copy(source.at[0, here], target.at[here], sems.at[which, part])

    wide_blocks, deep_blocks = width // BLOCK, cols // BLOCK
    for which in range(3):
        for part in range(parts):
            bring(which, part).start()
    zero = jnp.zeros((BLOCK, BLOCK), BF16)
    for which, ref in ((0, gate_out), (1, up_out)):
        for part in range(parts):
            bring(which, part).wait()

            @pl.loop(part * (wide_blocks // parts), (part + 1) * (wide_blocks // parts))
            def _(row):
                for col in range(deep_blocks):

                    @pl.when(mask[(which * wide_blocks + row) * deep_blocks + col] == 0)
                    def _():
                        ref[pl.ds(row * BLOCK, BLOCK), col * BLOCK : (col + 1) * BLOCK] = zero

    for part in range(parts):
        bring(2, part).wait()

    @pl.loop(0, wide_blocks)
    def _(row):
        for col in range(deep_blocks):

            @pl.when(mask[(2 * wide_blocks + row) * deep_blocks + col] == 0)
            def _():
                down_out[col * BLOCK : (col + 1) * BLOCK, pl.ds(row * BLOCK, BLOCK)] = zero


def forward_kernel(flags, *refs, peers, stage):
    pieces = refs[:peers]
    gain, gmat, umat, dmat = refs[peers : peers + 4]
    xval, gate_store, up_store, partial, normed, hidden = refs[peers + 7 :]
    part = pieces[0].shape[1]
    width, cols = gmat.shape
    tile = tile_of(cols)

    @pl.when(flags[0] == stage)
    def _():
        for step in range(peers):
            place = lax.rem(flags[1] + peers - step, peers) * part
            xval[:, pl.ds(pl.multiple_of(place, part), part)] = pieces[step][...]

        def square(index, total):
            here = xval[:, pl.ds(pl.multiple_of(index * part, part), part)].astype(F32)
            return total + jnp.sum(here * here, axis=1, keepdims=True)

        total = lax.fori_loop(0, peers, square, jnp.zeros((xval.shape[0], 1), F32))
        scale = lax.rsqrt(total / width + EPS)

        @pl.loop(0, peers)
        def _(index):
            here = pl.ds(pl.multiple_of(index * part, part), part)
            normed[:, here] = (xval[:, here].astype(F32) * scale * gain[:, here]).astype(BF16)

        @pl.loop(0, cols // tile)
        def _(index):
            here = pl.ds(pl.multiple_of(index * tile, tile), tile)
            gate = jnp.dot(normed[...], gmat[:, here], preferred_element_type=F32)
            upper = jnp.dot(normed[...], umat[:, here], preferred_element_type=F32)
            gate_store[:, here] = gate
            up_store[:, here] = upper
            hidden[:, here] = (gate * jax.nn.sigmoid(gate) * upper).astype(BF16)

        @pl.loop(0, peers)
        def _(index):
            here = pl.ds(pl.multiple_of(index * part, part), part)
            partial[index] = jnp.dot(
                hidden[...], dmat[:, here], preferred_element_type=F32
            ).astype(BF16)


def backward_kernel(flags, *refs, peers, stage):
    pieces = refs[:peers]
    gain, gmat, umat, dmat, xval, gate_store, up_store = refs[peers : peers + 7]
    cot, partial, dgate, dup = refs[peers + 8 :]
    part = pieces[0].shape[1]
    width, cols = gmat.shape
    rows = xval.shape[0]
    tile = tile_of(cols)

    @pl.when(flags[0] == stage)
    def _():
        for step in range(peers):
            place = lax.rem(flags[1] + peers - step, peers) * part
            cot[:, pl.ds(pl.multiple_of(place, part), part)] = pieces[step][...]

        def square(index, total):
            here = xval[:, pl.ds(pl.multiple_of(index * part, part), part)].astype(F32)
            return total + jnp.sum(here * here, axis=1, keepdims=True)

        total = lax.fori_loop(0, peers, square, jnp.zeros((rows, 1), F32))
        scale = lax.rsqrt(total / width + EPS)

        def hidden_side(index, inner):
            here = pl.ds(pl.multiple_of(index * tile, tile), tile)
            dhid = contract_last(cot[...], dmat[here, :])
            gate = gate_store[:, here]
            upper = up_store[:, here]
            sig = jax.nn.sigmoid(gate)
            dgate_low = (dhid * upper * sig * (1.0 + gate * (1.0 - sig))).astype(BF16)
            dup_low = (dhid * gate * sig).astype(BF16)
            dgate[:, here] = dgate_low
            dup[:, here] = dup_low
            both = dgate_low.astype(F32) * gate + dup_low.astype(F32) * upper
            return inner + jnp.sum(both, axis=1, keepdims=True)

        inner = lax.fori_loop(0, cols // tile, hidden_side, jnp.zeros((rows, 1), F32))
        pull = scale * scale * inner / width

        @pl.loop(0, peers)
        def _(index):
            here = pl.ds(pl.multiple_of(index * part, part), part)
            dnorm = contract_last(dgate[...], gmat[here, :]) + contract_last(dup[...], umat[here, :])
            back = scale * (dnorm * gain[:, here]) - xval[:, here].astype(F32) * pull
            partial[index] = back.astype(BF16)


def local(inputs, out_grad, norm_gain, gate_weight, up_weight, down_weight, block_mask):
    stages, peers = lax.axis_size("pipe"), lax.axis_size("tensor")
    stage, peer = lax.axis_index("pipe"), lax.axis_index("tensor")
    rows, part = inputs.shape
    width, cols = gate_weight.shape[1:]
    flags = jnp.stack([stage, peer]).astype(jnp.int32)
    vmem = functools.partial(pltpu.CompilerParams, vmem_limit_bytes=14 * 2**20)

    gmat, umat, dmat = pl.pallas_call(
        load_kernel,
        out_shape=(
            pltpu.VMEM((width, cols), BF16),
            pltpu.VMEM((width, cols), BF16),
            pltpu.VMEM((cols, width), BF16),
        ),
        in_specs=[SMEM_WHOLE] + [HBM_WHOLE] * 3,
        out_specs=(VMEM_WHOLE,) * 3,
        scratch_shapes=[pltpu.SemaphoreType.DMA((3, 4))],
        compiler_params=vmem(),
        cost_estimate=pl.CostEstimate(flops=0, bytes_accessed=6 * width * cols, transcendentals=0),
        name="load_masked",
    )(block_mask.reshape(-1), gate_weight, up_weight, down_weight)

    in_vmem = functools.partial(pltpu.with_memory_space_constraint, memory_space=pltpu.VMEM)
    weights = [in_vmem(weight) for weight in (gmat, umat, dmat)]
    cost = pl.CostEstimate(
        flops=6 * rows * width * cols, bytes_accessed=6 * width * cols, transcendentals=0
    )
    partial_type = jax.ShapeDtypeStruct((peers, rows, part), BF16)
    hidden_type = pltpu.VMEM((rows, cols), F32)
    wide_type = pltpu.VMEM((rows, width), BF16)

    def forward(at, pieces, kept):
        return pl.pallas_call(
            functools.partial(forward_kernel, peers=peers, stage=at),
            out_shape=(wide_type, hidden_type, hidden_type, partial_type),
            in_specs=[SMEM_WHOLE] + [VMEM_WHOLE] * (peers + 7),
            out_specs=(VMEM_WHOLE,) * 4,
            scratch_shapes=[pltpu.VMEM((rows, width), BF16), pltpu.VMEM((rows, cols), BF16)],
            input_output_aliases={peers + 5: 0, peers + 6: 1, peers + 7: 2},
            compiler_params=vmem(),
            cost_estimate=cost,
            name="forward_layer",
        )(flags, *map(in_vmem, pieces), in_vmem(norm_gain), *weights, *map(in_vmem, kept))

    def backward(at, pieces, kept, cot):
        return pl.pallas_call(
            functools.partial(backward_kernel, peers=peers, stage=at),
            out_shape=(wide_type, partial_type),
            in_specs=[SMEM_WHOLE] + [VMEM_WHOLE] * (peers + 8),
            out_specs=(VMEM_WHOLE,) * 2,
            scratch_shapes=[pltpu.VMEM((rows, cols), BF16), pltpu.VMEM((rows, cols), BF16)],
            input_output_aliases={peers + 8: 0},
            compiler_params=vmem(),
            cost_estimate=cost,
            name="backward_layer",
        )(flags, *map(in_vmem, pieces), in_vmem(norm_gain), *weights, *map(in_vmem, kept), in_vmem(cot))

    def number(at, who):
        return at * peers + who

    def spread(value, routes, include_self):
        return [
            lax.ppermute(
                value,
                ("pipe", "tensor"),
                [
                    (number(source, who), number(target, (who + step) % peers))
                    for source, target in routes
                    for who in range(peers)
                ],
            )
            if step or include_self
            else value
            for step in range(peers)
        ]

    def summed(partial, whole):
        own = lax.dynamic_slice_in_dim(whole, peer * part, part, 1)
        arrived = lax.all_to_all(partial, "tensor", 0, 0)
        return (own.astype(F32) + jnp.sum(arrived.astype(F32), axis=0)).astype(BF16)

    first = jnp.where(stage == stages - 1, out_grad, inputs)
    ends = spread(first, [(0, 0), (stages - 1, stages - 1)], False)
    pieces = ends
    kept = (
        jnp.zeros((rows, width), BF16),
        jnp.zeros((rows, cols), F32),
        jnp.zeros((rows, cols), F32),
    )
    for at in range(stages):
        *kept, partial = forward(at, pieces, kept)
        if at < stages - 1:
            pieces = spread(summed(partial, kept[0]), [(at, at + 1)], True)
    last_partial = partial
    cot = jnp.zeros((rows, width), BF16)
    pieces = ends
    for at in range(stages - 1, -1, -1):
        cot, partial = backward(at, pieces, kept, cot)
        if at > 0:
            pieces = spread(summed(partial, cot), [(at, at - 1)], True)

    final = stage == stages - 1
    ends = spread(
        summed(jnp.where(final, last_partial, partial), jnp.where(final, kept[0], cot)),
        [(0, 0), (stages - 1, stages - 1)],
        False,
    )
    order = (peer - jnp.arange(peers)) % peers
    end = jnp.zeros((rows, peers, part), BF16).at[:, order].set(jnp.stack(ends, 1))
    end = end.reshape(rows, width)
    onward = lax.ppermute(kept[0], "pipe", [(at + 1, at) for at in range(stages - 1)])
    back = lax.ppermute(cot, "pipe", [(at, at + 1) for at in range(stages - 1)])
    section_out = jnp.where(final, end, onward).astype(F32)
    section_grad = jnp.where(stage == 0, end, back).astype(F32)
    return section_out[None], section_grad[None]


def solution(mesh):
    in_specs = (
        P(None, "tensor"),
        P(None, "tensor"),
        P("pipe", None),
        P("pipe", None, "tensor"),
        P("pipe", None, "tensor"),
        P("pipe", "tensor", None),
        P("pipe", None, None, "tensor"),
    )
    out_specs = (P("pipe", None, None), P("pipe", None, None))
    return jax.shard_map(local, mesh=mesh, in_specs=in_specs, out_specs=out_specs, check_vma=False)
```

time: 1480 us -> 603 us (0.41); the launches traced: 1460 us -> 601 us
  waiting for transfers between devices: 931 us -> 49.1 us
  starting transfers between devices: 13.2 us -> 294 us
  matrix products: 229 us -> 0 us
  blocking collectives: 0 us -> 163 us
  local copies, waits for them, and re-layouts: 156 us -> 23.4 us
  other arithmetic: 119 us -> 9.59 us
  Pallas kernels: 0 us -> 60.4 us
    psum x10 -> x0, waiting for transfers between devices: 846 us -> none  [the longest x5 429 us: forward_step_once(): summed = lax.psum(partial_out, 'tensor')]
    ppermute x10 -> x64, starting transfers between devices: 13.1 us -> 290 us  [the longest x62 276 us: spread(): lax.ppermute(value, ('pipe', 'tensor'), [(number(source, who), number(tar...]
    dot_general x30 -> x0, matrix products: 229 us -> none  [the longest x15 153 us: contract_last(): lax.dot_general(left, right, (((1,), (1,)), ((), ())), preferred_element_...]
    all_to_all x0 -> x6, blocking collectives: none -> 163 us  [summed(): arrived = lax.all_to_all(partial, 'tensor', 0, 0)]
    pallas_call x0 -> x9, Pallas kernels: none -> 60.4 us  [the longest x4 24.6 us: backward(): pl.pallas_call(functools.partial(backward_kernel, peers=peers, stage=at),...]
    mul x3 -> x0, other arithmetic: 57.8 us -> none  [masked_blocks(): shaped * mask.astype(weight.dtype)[:, None, :, None]]
    all_gather x2 -> x0, waiting for transfers between devices: 53.8 us -> none  [the longest x1 53.8 us: local(): lax.all_gather(out_grad, 'tensor', axis=1, tiled=True)]
    while x182 -> x0, local copies, waits for them, and re-layouts: 52 us -> none  [the longest x2 37.5 us: local(): lax.fori_loop(0, step_total, forward_step_once, first_position)]
  transfers between devices with their start and end apart: 22 -> 65, of which waited for: 21 -> 10; matrix products, arithmetic and copies ran while one was open for 12% -> 1% of each run, Pallas kernels for 0% -> 3%
where the time goes in v1:
time: 603 us; the launch traced here: 601 us
  starting transfers between devices  294 us (49%)
  blocking collectives  163 us (27%)
  Pallas kernels  60.4 us (10%)
  waiting for transfers between devices  49.1 us (8%)
  local copies, waits for them, and re-layouts  23.4 us (4%)
  other arithmetic  9.59 us (2%)
    ppermute x62, starting transfers between devices, spread(): lax.ppermute(value, ('pipe', 'tensor'), [(number(source, who), number(tar...  276 us
    all_to_all x6, blocking collectives, summed(): arrived = lax.all_to_all(partial, 'tensor', 0, 0)  163 us
    ppermute x62, waiting for transfers between devices, spread(): lax.ppermute(value, ('pipe', 'tensor'), [(number(source, who), number(tar...  32.7 us
    pallas_call x4, Pallas kernels, backward(): pl.pallas_call(functools.partial(backward_kernel, peers=peers, stage=at),...  24.6 us
    unnamed x49, local copies, waits for them, and re-layouts  21.3 us
    pallas_call x1, Pallas kernels, local(): pl.pallas_call(load_kernel, out_shape=(pltpu.VMEM((width, cols), BF16), p...  19.2 us
    pallas_call x4, Pallas kernels, forward(): pl.pallas_call(functools.partial(forward_kernel, peers=peers, stage=at),...  16.5 us
    all_to_all x1, waiting for transfers between devices, summed(): arrived = lax.all_to_all(partial, 'tensor', 0, 0)  16.4 us
  transfers between devices with their start and end apart: 65, of which 10 were waited for; matrix products, arithmetic and copies ran while one was open for 1% of the time, Pallas kernels for 3%

profile of v1, /device:TPU:0, one launch (start us, length us, event | category | flops | bytes accessed | tf_op | source)
XLA Modules:
  0.0 601.1 jit_solution(3886077877033209485)
XLA Ops:
  30.3 19.2 %load_masked.1 = (bf16[4096,1792]{1,0:T(8,128)(2,1)S(1)}, bf16[4096,1792]{1,0:T(8,128)(2,1)S(1)}, bf16[1792,4096]{1,0:T(8,128)(2,1)S(1)}) custom-call(s32[1344]{0:T(1024)} %reshape.59.mask, bf16[1,4096,1792]{2,1,0:T(8,128)(2,1)} %gate_hbm.1, bf16[1,4096,1792]{2,1,0:T(8,128)(2,1)} %up_hbm.1, bf16[1,1792,4096]{2,1,0:T(8,128)(2,1)} %down_hbm.1), custom_call_target="tpu_custom_call" | custom-call | bytes 44040192 | tf_op jit(solution)/shard_map/load_masked/pallas_call | solution.py:164
  55.4 11.4 %forward_layer.4 = (bf16[128,4096]{1,0:T(8,128)(2,1)S(1)}, f32[128,1792]{1,0:T(8,128)S(1)}, f32[128,1792]{1,0:T(8,128)S(1)}, bf16[8,128,512]{2,1,0:T(8,128)(2,1)}) custom-call(s32[2]{0:T(128)} %pad_add_fusion.flags, bf16[128,512]{1,0:T(8,128)(2,1)S(1)} %broadcast_select_fusion.1.refs_0_, ...), custom_call_target="tpu_custom_call", output_to_operand_aliasing={{0}: (13, {}), {1}: (14, {}), {2}: (15, {})} | custom-call | flops 5637144576 | bytes 44040192 | tf_op jit(solution)/shard_map/forward_layer/pallas_call | solution.py:189
  71.2 16.4 %all-to-all-done = bf16[8,128,512]{2,1,0:T(8,128)(2,1)} async-done(((bf16[8,128,512]{2,1,0:T(8,128)(2,1)}), bf16[8,128,512]{2,1,0:T(8,128)(2,1)}, u32[]{:S(2)}, u32[]{:S(2)}) %all-to-all-start) | async-done | bytes 1048608 | tf_op jit(solution)/shard_map/all_to_all | solution.py:235
  120.5 25.2 %all_to_all.35 = bf16[8,128,512]{2,1,0:T(8,128)(2,1)S(1)} all-to-all(bf16[8,128,512]{2,1,0:T(8,128)(2,1)} %get-tuple-element.37), channel_id=1, replica_groups=mesh['pipe'=4,'tensor'=8] {'tensor'}, dimensions={0} | all-to-all | bytes 2097152 | tf_op jit(solution)/shard_map/all_to_all | solution.py:235
  153.0 30.3 %all_to_all.36 = bf16[8,128,512]{2,1,0:T(8,128)(2,1)S(1)} all-to-all(bf16[8,128,512]{2,1,0:T(8,128)(2,1)} %get-tuple-element.41), channel_id=1, replica_groups=mesh['pipe'=4,'tensor'=8] {'tensor'}, dimensions={0} | all-to-all | bytes 2097152 | tf_op jit(solution)/shard_map/all_to_all | solution.py:235
  183.6 34.1 %collective-permute-start.23 = (bf16[128,512]{1,0:T(8,128)(2,1)S(1)}, bf16[128,512]{1,0:T(8,128)(2,1)S(1)}, u32[]{:S(2)}, u32[]{:S(2)}) collective-permute-start(bf16[128,512]{1,0:T(8,128)(2,1)S(1)} %add_convert_fusion.4), channel_id=1, source_target_pairs={{16,24},{17,25},{18,26},{19,27},{20,28},{21,29},{22,30},{23,31}} | collective-permute-start | bytes 393224 | tf_op jit(solution)/shard_map/ppermute | solution.py:219
  217.7 7.0 %collective-permute-start.24 = (bf16[128,512]{1,0:T(8,128)(2,1)S(1)}, bf16[128,512]{1,0:T(8,128)(2,1)S(1)}, u32[]{:S(2)}, u32[]{:S(2)}) collective-permute-start(bf16[128,512]{1,0:T(8,128)(2,1)S(1)} %add_convert_fusion.4), channel_id=1, source_target_pairs={{16,25},{17,26},{18,27},{19,28},{20,29},{21,30},{22,31},{23,24}} | collective-permute-start | bytes 393224 | tf_op jit(solution)/shard_map/ppermute | solution.py:219
  224.7 7.0 %collective-permute-start.25 = (bf16[128,512]{1,0:T(8,128)(2,1)S(1)}, bf16[128,512]{1,0:T(8,128)(2,1)S(1)}, u32[]{:S(2)}, u32[]{:S(2)}) collective-permute-start(bf16[128,512]{1,0:T(8,128)(2,1)S(1)} %add_convert_fusion.4), channel_id=1, source_target_pairs={{16,26},{17,27},{18,28},{19,29},{20,30},{21,31},{22,24},{23,25}} | collective-permute-start | bytes 393224 | tf_op jit(solution)/shard_map/ppermute | solution.py:219
  231.7 7.0 %collective-permute-start.26 = (bf16[128,512]{1,0:T(8,128)(2,1)S(1)}, bf16[128,512]{1,0:T(8,128)(2,1)S(1)}, u32[]{:S(2)}, u32[]{:S(2)}) collective-permute-start(bf16[128,512]{1,0:T(8,128)(2,1)S(1)} %add_convert_fusion.4), channel_id=1, source_target_pairs={{16,27},{17,28},{18,29},{19,30},{20,31},{21,24},{22,25},{23,26}} | collective-permute-start | bytes 393224 | tf_op jit(solution)/shard_map/ppermute | solution.py:219
  238.7 7.0 %collective-permute-start.27 = (bf16[128,512]{1,0:T(8,128)(2,1)S(1)}, bf16[128,512]{1,0:T(8,128)(2,1)S(1)}, u32[]{:S(2)}, u32[]{:S(2)}) collective-permute-start(bf16[128,512]{1,0:T(8,128)(2,1)S(1)} %add_convert_fusion.4), channel_id=1, source_target_pairs={{16,28},{17,29},{18,30},{19,31},{20,24},{21,25},{22,26},{23,27}} | collective-permute-start | bytes 393224 | tf_op jit(solution)/shard_map/ppermute | solution.py:219
  245.8 7.0 %collective-permute-start.28 = (bf16[128,512]{1,0:T(8,128)(2,1)S(1)}, bf16[128,512]{1,0:T(8,128)(2,1)S(1)}, u32[]{:S(2)}, u32[]{:S(2)}) collective-permute-start(bf16[128,512]{1,0:T(8,128)(2,1)S(1)} %add_convert_fusion.4), channel_id=1, source_target_pairs={{16,29},{17,30},{18,31},{19,24},{20,25},{21,26},{22,27},{23,28}} | collective-permute-start | bytes 393224 | tf_op jit(solution)/shard_map/ppermute | solution.py:219
  252.8 7.0 %collective-permute-start.29 = (bf16[128,512]{1,0:T(8,128)(2,1)S(1)}, bf16[128,512]{1,0:T(8,128)(2,1)S(1)}, u32[]{:S(2)}, u32[]{:S(2)}) collective-permute-start(bf16[128,512]{1,0:T(8,128)(2,1)S(1)} %add_convert_fusion.4), channel_id=1, source_target_pairs={{16,30},{17,31},{18,24},{19,25},{20,26},{21,27},{22,28},{23,29}} | collective-permute-start | bytes 393224 | tf_op jit(solution)/shard_map/ppermute | solution.py:219
  259.8 7.0 %collective-permute-start.30 = (bf16[128,512]{1,0:T(8,128)(2,1)S(1)}, bf16[128,512]{1,0:T(8,128)(2,1)S(1)}, u32[]{:S(2)}, u32[]{:S(2)}) collective-permute-start(bf16[128,512]{1,0:T(8,128)(2,1)S(1)} %add_convert_fusion.4), channel_id=1, source_target_pairs={{16,31},{17,24},{18,25},{19,26},{20,27},{21,28},{22,29},{23,30}} | collective-permute-start | bytes 393224 | tf_op jit(solution)/shard_map/ppermute | solution.py:219
  270.5 32.0 %all_to_all.37 = bf16[8,128,512]{2,1,0:T(8,128)(2,1)S(1)} all-to-all(bf16[8,128,512]{2,1,0:T(8,128)(2,1)} %get-tuple-element.48), channel_id=1, replica_groups=mesh['pipe'=4,'tensor'=8] {'tensor'}, dimensions={0} | all-to-all | bytes 2097152 | tf_op jit(solution)/shard_map/all_to_all | solution.py:235
  302.7 23.7 %collective-permute-start.31 = (bf16[128,512]{1,0:T(8,128)(2,1)S(1)}, bf16[128,512]{1,0:T(8,128)(2,1)S(1)}, u32[]{:S(2)}, u32[]{:S(2)}) collective-permute-start(bf16[128,512]{1,0:T(8,128)(2,1)S(1)} %add_convert_fusion.3), channel_id=1, source_target_pairs={{24,16},{25,17},{26,18},{27,19},{28,20},{29,21},{30,22},{31,23}} | collective-permute-start | bytes 393224 | tf_op jit(solution)/shard_map/ppermute | solution.py:219
  375.7 32.0 %all_to_all.38 = bf16[8,128,512]{2,1,0:T(8,128)(2,1)S(1)} all-to-all(bf16[8,128,512]{2,1,0:T(8,128)(2,1)} %get-tuple-element.50), channel_id=1, replica_groups=mesh['pipe'=4,'tensor'=8] {'tensor'}, dimensions={0} | all-to-all | bytes 2097152 | tf_op jit(solution)/shard_map/all_to_all | solution.py:235
  410.5 17.8 %collective-permute-start.43 = (bf16[128,512]{1,0:T(8,128)(2,1)S(1)}, bf16[128,512]{1,0:T(8,128)(2,1)S(1)}, u32[]{:S(2)}, u32[]{:S(2)}) collective-permute-start(bf16[128,512]{1,0:T(8,128)(2,1)S(1)} %add_convert_fusion.2), channel_id=1, source_target_pairs={{16,12},{17,13},{18,14},{19,15},{20,8},{21,9},{22,10},{23,11}} | collective-permute-start | bytes 393224 | tf_op jit(solution)/shard_map/ppermute | solution.py:219
  435.4 7.0 %collective-permute-start.45 = (bf16[128,512]{1,0:T(8,128)(2,1)S(1)}, bf16[128,512]{1,0:T(8,128)(2,1)S(1)}, u32[]{:S(2)}, u32[]{:S(2)}) collective-permute-start(bf16[128,512]{1,0:T(8,128)(2,1)S(1)} %add_convert_fusion.2), channel_id=1, source_target_pairs={{16,14},{17,15},{18,8},{19,9},{20,10},{21,11},{22,12},{23,13}} | collective-permute-start | bytes 393224 | tf_op jit(solution)/shard_map/ppermute | solution.py:219
  442.4 7.0 %collective-permute-start.46 = (bf16[128,512]{1,0:T(8,128)(2,1)S(1)}, bf16[128,512]{1,0:T(8,128)(2,1)S(1)}, u32[]{:S(2)}, u32[]{:S(2)}) collective-permute-start(bf16[128,512]{1,0:T(8,128)(2,1)S(1)} %add_convert_fusion.2), channel_id=1, source_target_pairs={{16,15},{17,8},{18,9},{19,10},{20,11},{21,12},{22,13},{23,14}} | collective-permute-start | bytes 393224 | tf_op jit(solution)/shard_map/ppermute | solution.py:219
  451.2 21.9 %all_to_all.39 = bf16[8,128,512]{2,1,0:T(8,128)(2,1)S(1)} all-to-all(bf16[8,128,512]{2,1,0:T(8,128)(2,1)} %get-tuple-element.52), channel_id=1, replica_groups=mesh['pipe'=4,'tensor'=8] {'tensor'}, dimensions={0} | all-to-all | bytes 2097152 | tf_op jit(solution)/shard_map/all_to_all | solution.py:235
  479.9 16.9 %collective-permute-done.47.refs_0_ = bf16[128,512]{1,0:T(8,128)(2,1)S(1)} collective-permute-done((bf16[128,512]{1,0:T(8,128)(2,1)S(1)}, bf16[128,512]{1,0:T(8,128)(2,1)S(1)}, u32[]{:S(2)}, u32[]{:S(2)}) %collective-permute-start.47) | collective-permute-done | bytes 131104 | tf_op jit(solution)/shard_map/ppermute | solution.py:219
  510.4 19.5 %backward_layer.7 = (bf16[128,4096]{1,0:T(8,128)(2,1)S(1)}, bf16[8,128,512]{2,1,0:T(8,128)(2,1)}) custom-call(s32[2]{0:T(128)} %pad_add_fusion.flags, bf16[128,512]{1,0:T(8,128)(2,1)S(1)} %collective-permute-done.47.refs_0_, bf16[128,512]{1,0:T(8,128)(2,1)S(1)} %collective-permute-done.48.refs_1_, ...), custom_call_target="tpu_custom_call", output_to_operand_aliasing={{0}: (16, {})} | custom-call | flops 5637144576 | bytes 44040192 | tf_op jit(solution)/shard_map/backward_layer/pallas_call | solution.py:202
  531.7 21.5 %all_to_all.40 = bf16[8,128,512]{2,1,0:T(8,128)(2,1)S(1)} all-to-all(bf16[8,128,512]{2,1,0:T(8,128)(2,1)S(1)} %broadcast_select_fusion), channel_id=1, replica_groups=mesh['pipe'=4,'tensor'=8] {'tensor'}, dimensions={0} | all-to-all | bytes 2097152 | tf_op jit(solution)/shard_map/all_to_all | solution.py:235
  560.9 9.4 %collective-permute-start.63 = (bf16[128,4096]{1,0:T(8,128)(2,1)}, bf16[128,4096]{1,0:T(8,128)(2,1)}, u32[]{:S(2)}, u32[]{:S(2)}) collective-permute-start(bf16[128,4096]{1,0:T(8,128)(2,1)} %copy-done.6), channel_id=1, source_target_pairs={{0,8},{8,16},{16,24},{1,9},{9,17},{17,25},{2,10},{10,18},{18,26},{... | collective-permute-start | bytes 3145736 | tf_op jit(solution)/shard_map/ppermute | solution.py:268
  (198 shorter events, 204.8 us)
Async XLA Ops:
  9.9 40.4 %collective-permute-start.2 = (bf16[128,512]{1,0:T(8,128)(2,1)S(1)}, bf16[128,512]{1,0:T(8,128)(2,1)S(1)}, u32[]{:S(2)}, u32[]{:S(2)}) collective-permute-start(bf16[128,512]{1,0:T(8,128)(2,1)S(1)} %broadcast_select_fusion.1.refs_0_), channel_id=1, source_target_pairs={{0,3},{1,4},{2,5},{3,6},{4,7},{5,0},{6,1},{7,2},{24,27},{25,28},{2... | collective-permute-start | bytes 393224 | tf_op jit(solution)/shard_map/ppermute | solution.py:219
  14.4 35.9 %collective-permute-start.3 = (bf16[128,512]{1,0:T(8,128)(2,1)S(1)}, bf16[128,512]{1,0:T(8,128)(2,1)S(1)}, u32[]{:S(2)}, u32[]{:S(2)}) collective-permute-start(bf16[128,512]{1,0:T(8,128)(2,1)S(1)} %broadcast_select_fusion.1.refs_0_), channel_id=1, source_target_pairs={{0,4},{1,5},{2,6},{3,7},{4,0},{5,1},{6,2},{7,3},{24,28},{25,29},{2... | collective-permute-start | bytes 393224 | tf_op jit(solution)/shard_map/ppermute | solution.py:219
  17.5 33.9 %collective-permute-start.4 = (bf16[128,512]{1,0:T(8,128)(2,1)S(1)}, bf16[128,512]{1,0:T(8,128)(2,1)S(1)}, u32[]{:S(2)}, u32[]{:S(2)}) collective-permute-start(bf16[128,512]{1,0:T(8,128)(2,1)S(1)} %broadcast_select_fusion.1.refs_0_), channel_id=1, source_target_pairs={{0,5},{1,6},{2,7},{3,0},{4,1},{5,2},{6,3},{7,4},{24,29},{25,30},{2... | collective-permute-start | bytes 393224 | tf_op jit(solution)/shard_map/ppermute | solution.py:219
  22.1 30.7 %collective-permute-start.5 = (bf16[128,512]{1,0:T(8,128)(2,1)S(1)}, bf16[128,512]{1,0:T(8,128)(2,1)S(1)}, u32[]{:S(2)}, u32[]{:S(2)}) collective-permute-start(bf16[128,512]{1,0:T(8,128)(2,1)S(1)} %broadcast_select_fusion.1.refs_0_), channel_id=1, source_target_pairs={{0,6},{1,7},{2,0},{3,1},{4,2},{5,3},{6,4},{7,5},{24,30},{25,31},{2... | collective-permute-start | bytes 393224 | tf_op jit(solution)/shard_map/ppermute | solution.py:219
  25.4 28.1 %collective-permute-start.6 = (bf16[128,512]{1,0:T(8,128)(2,1)S(1)}, bf16[128,512]{1,0:T(8,128)(2,1)S(1)}, u32[]{:S(2)}, u32[]{:S(2)}) collective-permute-start(bf16[128,512]{1,0:T(8,128)(2,1)S(1)} %broadcast_select_fusion.1.refs_0_), channel_id=1, source_target_pairs={{0,7},{1,0},{2,1},{3,2},{4,3},{5,4},{6,5},{7,6},{24,31},{25,24},{2... | collective-permute-start | bytes 393224 | tf_op jit(solution)/shard_map/ppermute | solution.py:219
  183.6 62.2 %collective-permute-start.23 = (bf16[128,512]{1,0:T(8,128)(2,1)S(1)}, bf16[128,512]{1,0:T(8,128)(2,1)S(1)}, u32[]{:S(2)}, u32[]{:S(2)}) collective-permute-start(bf16[128,512]{1,0:T(8,128)(2,1)S(1)} %add_convert_fusion.4), channel_id=1, source_target_pairs={{16,24},{17,25},{18,26},{19,27},{20,28},{21,29},{22,30},{23,31}} | collective-permute-start | bytes 393224 | tf_op jit(solution)/shard_map/ppermute | solution.py:219
  217.7 35.1 %collective-permute-start.24 = (bf16[128,512]{1,0:T(8,128)(2,1)S(1)}, bf16[128,512]{1,0:T(8,128)(2,1)S(1)}, u32[]{:S(2)}, u32[]{:S(2)}) collective-permute-start(bf16[128,512]{1,0:T(8,128)(2,1)S(1)} %add_convert_fusion.4), channel_id=1, source_target_pairs={{16,25},{17,26},{18,27},{19,28},{20,29},{21,30},{22,31},{23,24}} | collective-permute-start | bytes 393224 | tf_op jit(solution)/shard_map/ppermute | solution.py:219
  224.7 35.1 %collective-permute-start.25 = (bf16[128,512]{1,0:T(8,128)(2,1)S(1)}, bf16[128,512]{1,0:T(8,128)(2,1)S(1)}, u32[]{:S(2)}, u32[]{:S(2)}) collective-permute-start(bf16[128,512]{1,0:T(8,128)(2,1)S(1)} %add_convert_fusion.4), channel_id=1, source_target_pairs={{16,26},{17,27},{18,28},{19,29},{20,30},{21,31},{22,24},{23,25}} | collective-permute-start | bytes 393224 | tf_op jit(solution)/shard_map/ppermute | solution.py:219
  231.7 35.1 %collective-permute-start.26 = (bf16[128,512]{1,0:T(8,128)(2,1)S(1)}, bf16[128,512]{1,0:T(8,128)(2,1)S(1)}, u32[]{:S(2)}, u32[]{:S(2)}) collective-permute-start(bf16[128,512]{1,0:T(8,128)(2,1)S(1)} %add_convert_fusion.4), channel_id=1, source_target_pairs={{16,27},{17,28},{18,29},{19,30},{20,31},{21,24},{22,25},{23,26}} | collective-permute-start | bytes 393224 | tf_op jit(solution)/shard_map/ppermute | solution.py:219
  238.7 28.1 %collective-permute-start.27 = (bf16[128,512]{1,0:T(8,128)(2,1)S(1)}, bf16[128,512]{1,0:T(8,128)(2,1)S(1)}, u32[]{:S(2)}, u32[]{:S(2)}) collective-permute-start(bf16[128,512]{1,0:T(8,128)(2,1)S(1)} %add_convert_fusion.4), channel_id=1, source_target_pairs={{16,28},{17,29},{18,30},{19,31},{20,24},{21,25},{22,26},{23,27}} | collective-permute-start | bytes 393224 | tf_op jit(solution)/shard_map/ppermute | solution.py:219
  302.7 50.8 %collective-permute-start.31 = (bf16[128,512]{1,0:T(8,128)(2,1)S(1)}, bf16[128,512]{1,0:T(8,128)(2,1)S(1)}, u32[]{:S(2)}, u32[]{:S(2)}) collective-permute-start(bf16[128,512]{1,0:T(8,128)(2,1)S(1)} %add_convert_fusion.3), channel_id=1, source_target_pairs={{24,16},{25,17},{26,18},{27,19},{28,20},{29,21},{30,22},{31,23}} | collective-permute-start | bytes 393224 | tf_op jit(solution)/shard_map/ppermute | solution.py:219
  326.3 33.9 %collective-permute-start.32 = (bf16[128,512]{1,0:T(8,128)(2,1)S(1)}, bf16[128,512]{1,0:T(8,128)(2,1)S(1)}, u32[]{:S(2)}, u32[]{:S(2)}) collective-permute-start(bf16[128,512]{1,0:T(8,128)(2,1)S(1)} %add_convert_fusion.3), channel_id=1, source_target_pairs={{24,17},{25,18},{26,19},{27,20},{28,21},{29,22},{30,23},{31,16}} | collective-permute-start | bytes 393224 | tf_op jit(solution)/shard_map/ppermute | solution.py:219
  333.1 33.9 %collective-permute-start.33 = (bf16[128,512]{1,0:T(8,128)(2,1)S(1)}, bf16[128,512]{1,0:T(8,128)(2,1)S(1)}, u32[]{:S(2)}, u32[]{:S(2)}) collective-permute-start(bf16[128,512]{1,0:T(8,128)(2,1)S(1)} %add_convert_fusion.3), channel_id=1, source_target_pairs={{24,18},{25,19},{26,20},{27,21},{28,22},{29,23},{30,16},{31,17}} | collective-permute-start | bytes 393224 | tf_op jit(solution)/shard_map/ppermute | solution.py:219
  339.9 33.9 %collective-permute-start.34 = (bf16[128,512]{1,0:T(8,128)(2,1)S(1)}, bf16[128,512]{1,0:T(8,128)(2,1)S(1)}, u32[]{:S(2)}, u32[]{:S(2)}) collective-permute-start(bf16[128,512]{1,0:T(8,128)(2,1)S(1)} %add_convert_fusion.3), channel_id=1, source_target_pairs={{24,19},{25,20},{26,21},{27,22},{28,23},{29,16},{30,17},{31,18}} | collective-permute-start | bytes 393224 | tf_op jit(solution)/shard_map/ppermute | solution.py:219
  346.7 27.1 %collective-permute-start.35 = (bf16[128,512]{1,0:T(8,128)(2,1)S(1)}, bf16[128,512]{1,0:T(8,128)(2,1)S(1)}, u32[]{:S(2)}, u32[]{:S(2)}) collective-permute-start(bf16[128,512]{1,0:T(8,128)(2,1)S(1)} %add_convert_fusion.3), channel_id=1, source_target_pairs={{24,20},{25,21},{26,22},{27,23},{28,16},{29,17},{30,18},{31,19}} | collective-permute-start | bytes 393224 | tf_op jit(solution)/shard_map/ppermute | solution.py:219
  409.2 33.3 %collective-permute-start.41 = (bf16[128,512]{1,0:T(8,128)(2,1)S(1)}, bf16[128,512]{1,0:T(8,128)(2,1)S(1)}, u32[]{:S(2)}, u32[]{:S(2)}) collective-permute-start(bf16[128,512]{1,0:T(8,128)(2,1)S(1)} %add_convert_fusion.2), channel_id=1, source_target_pairs={{16,10},{17,11},{18,12},{19,13},{20,14},{21,15},{22,8},{23,9}} | collective-permute-start | bytes 393224 | tf_op jit(solution)/shard_map/ppermute | solution.py:219
  409.9 39.6 %collective-permute-start.42 = (bf16[128,512]{1,0:T(8,128)(2,1)S(1)}, bf16[128,512]{1,0:T(8,128)(2,1)S(1)}, u32[]{:S(2)}, u32[]{:S(2)}) collective-permute-start(bf16[128,512]{1,0:T(8,128)(2,1)S(1)} %add_convert_fusion.2), channel_id=1, source_target_pairs={{16,11},{17,12},{18,13},{19,14},{20,15},{21,8},{22,9},{23,10}} | collective-permute-start | bytes 393224 | tf_op jit(solution)/shard_map/ppermute | solution.py:219
  410.5 38.9 %collective-permute-start.43 = (bf16[128,512]{1,0:T(8,128)(2,1)S(1)}, bf16[128,512]{1,0:T(8,128)(2,1)S(1)}, u32[]{:S(2)}, u32[]{:S(2)}) collective-permute-start(bf16[128,512]{1,0:T(8,128)(2,1)S(1)} %add_convert_fusion.2), channel_id=1, source_target_pairs={{16,12},{17,13},{18,14},{19,15},{20,8},{21,9},{22,10},{23,11}} | collective-permute-start | bytes 393224 | tf_op jit(solution)/shard_map/ppermute | solution.py:219
  474.7 27.1 %collective-permute-start.48 = (bf16[128,512]{1,0:T(8,128)(2,1)S(1)}, bf16[128,512]{1,0:T(8,128)(2,1)S(1)}, u32[]{:S(2)}, u32[]{:S(2)}) collective-permute-start(bf16[128,512]{1,0:T(8,128)(2,1)S(1)} %add_convert_fusion.1), channel_id=1, source_target_pairs={{8,1},{9,2},{10,3},{11,4},{12,5},{13,6},{14,7},{15,0}} | collective-permute-start | bytes 393224 | tf_op jit(solution)/shard_map/ppermute | solution.py:219
  476.0 27.1 %collective-permute-start.49 = (bf16[128,512]{1,0:T(8,128)(2,1)S(1)}, bf16[128,512]{1,0:T(8,128)(2,1)S(1)}, u32[]{:S(2)}, u32[]{:S(2)}) collective-permute-start(bf16[128,512]{1,0:T(8,128)(2,1)S(1)} %add_convert_fusion.1), channel_id=1, source_target_pairs={{8,2},{9,3},{10,4},{11,5},{12,6},{13,7},{14,0},{15,1}} | collective-permute-start | bytes 393224 | tf_op jit(solution)/shard_map/ppermute | solution.py:219
  477.3 30.2 %collective-permute-start.50 = (bf16[128,512]{1,0:T(8,128)(2,1)S(1)}, bf16[128,512]{1,0:T(8,128)(2,1)S(1)}, u32[]{:S(2)}, u32[]{:S(2)}) collective-permute-start(bf16[128,512]{1,0:T(8,128)(2,1)S(1)} %add_convert_fusion.1), channel_id=1, source_target_pairs={{8,3},{9,4},{10,5},{11,6},{12,7},{13,0},{14,1},{15,2}} | collective-permute-start | bytes 393224 | tf_op jit(solution)/shard_map/ppermute | solution.py:219
  478.6 29.2 %collective-permute-start.51 = (bf16[128,512]{1,0:T(8,128)(2,1)S(1)}, bf16[128,512]{1,0:T(8,128)(2,1)S(1)}, u32[]{:S(2)}, u32[]{:S(2)}) collective-permute-start(bf16[128,512]{1,0:T(8,128)(2,1)S(1)} %add_convert_fusion.1), channel_id=1, source_target_pairs={{8,4},{9,5},{10,6},{11,7},{12,0},{13,1},{14,2},{15,3}} | collective-permute-start | bytes 393224 | tf_op jit(solution)/shard_map/ppermute | solution.py:219
  556.8 40.6 %collective-permute-start.62 = (bf16[128,4096]{1,0:T(8,128)(2,1)S(1)}, bf16[128,4096]{1,0:T(8,128)(2,1)}, u32[]{:S(2)}, u32[]{:S(2)}) collective-permute-start(bf16[128,4096]{1,0:T(8,128)(2,1)S(1)} %get-tuple-element.44.refs_12_), channel_id=1, source_target_pairs={{8,0},{16,8},{24,16},{9,1},{17,9},{25,17},{10,2},{18,10},{26,18},{... | collective-permute-start | bytes 3145736 | tf_op jit(solution)/shard_map/ppermute | solution.py:267
  560.9 36.5 %collective-permute-start.63 = (bf16[128,4096]{1,0:T(8,128)(2,1)}, bf16[128,4096]{1,0:T(8,128)(2,1)}, u32[]{:S(2)}, u32[]{:S(2)}) collective-permute-start(bf16[128,4096]{1,0:T(8,128)(2,1)} %copy-done.6), channel_id=1, source_target_pairs={{0,8},{8,16},{16,24},{1,9},{9,17},{17,25},{2,10},{10,18},{18,26},{... | collective-permute-start | bytes 3145736 | tf_op jit(solution)/shard_map/ppermute | solution.py:268
  (62 other events, 606.9 us)

commit v2 on v1

v2 whole, which is shorter than its diff:
```python
import functools

import jax
import jax.numpy as jnp
from jax import lax
from jax.experimental import pallas as pl
from jax.experimental.pallas import tpu as pltpu
from jax.sharding import PartitionSpec as P

BLOCK = 128
EPS = 1e-05
F32 = jnp.float32
BF16 = jnp.bfloat16
VMEM_WHOLE = pl.BlockSpec(memory_space=pltpu.VMEM)
SMEM_WHOLE = pl.BlockSpec(memory_space=pltpu.SMEM)
HBM_WHOLE = pl.BlockSpec(memory_space=pltpu.HBM)


def tile_of(size):
    return next(tile for tile in (256, 128) if size % tile == 0)


def load_kernel(mask, gate_hbm, up_hbm, down_hbm, *refs):
    gate_out, up_out, down_out, sems = refs[-4:]
    width, cols = gate_out.shape
    parts = sems.shape[1]
    wide_rows, deep_rows = width // parts, cols // parts

    def bring(which, part):
        source, target = ((gate_hbm, gate_out), (up_hbm, up_out), (down_hbm, down_out))[which]
        size = deep_rows if which == 2 else wide_rows
        here = pl.ds(part * size, size)
        return pltpu.make_async_copy(source.at[0, here], target.at[here], sems.at[which, part])

    wide_blocks, deep_blocks = width // BLOCK, cols // BLOCK
    for which in range(3):
        for part in range(parts):
            bring(which, part).start()
    zero = jnp.zeros((BLOCK, BLOCK), BF16)
    for which, ref in ((0, gate_out), (1, up_out)):
        for part in range(parts):
            bring(which, part).wait()

            @pl.loop(part * (wide_blocks // parts), (part + 1) * (wide_blocks // parts))
            def _(row):
                for col in range(deep_blocks):

                    @pl.when(mask[(which * wide_blocks + row) * deep_blocks + col] == 0)
                    def _():
                        ref[pl.ds(row * BLOCK, BLOCK), col * BLOCK : (col + 1) * BLOCK] = zero

    for part in range(parts):
        bring(2, part).wait()

    @pl.loop(0, wide_blocks)
    def _(row):
        for col in range(deep_blocks):

            @pl.when(mask[(2 * wide_blocks + row) * deep_blocks + col] == 0)
            def _():
                down_out[col * BLOCK : (col + 1) * BLOCK, pl.ds(row * BLOCK, BLOCK)] = zero


def place_pieces(flags, pieces, peers, part, store):
    for index in range(peers):
        if len(pieces) == 1:
            store(index * part, pieces[0][index])
        else:
            place = lax.rem(flags[1] + peers - index, peers) * part
            store(pl.multiple_of(place, part), pieces[index][...])


def forward_kernel(flags, *refs, peers, stage, count):
    pieces = refs[:count]
    gain, gmat, umat, dmat = refs[count : count + 4]
    xval, gate_store, up_store, partial, normed, hidden = refs[-6:]
    part = pieces[0].shape[-1]
    width, cols = gmat.shape
    tile = tile_of(cols)

    @pl.when(flags[0] == stage)
    def _():
        def store(place, value):
            xval[:, pl.ds(place, part)] = value

        place_pieces(flags, pieces, peers, part, store)

        def square(index, total):
            here = xval[:, pl.ds(pl.multiple_of(index * part, part), part)].astype(F32)
            return total + jnp.sum(here * here, axis=1, keepdims=True)

        total = lax.fori_loop(0, peers, square, jnp.zeros((xval.shape[0], 1), F32))
        scale = lax.rsqrt(total / width + EPS)

        @pl.loop(0, peers)
        def _(index):
            here = pl.ds(pl.multiple_of(index * part, part), part)
            normed[:, here] = (xval[:, here].astype(F32) * scale * gain[:, here]).astype(BF16)

        @pl.loop(0, cols // tile)
        def _(index):
            here = pl.ds(pl.multiple_of(index * tile, tile), tile)
            gate = jnp.dot(normed[...], gmat[:, here], preferred_element_type=F32)
            upper = jnp.dot(normed[...], umat[:, here], preferred_element_type=F32)
            gate_store[:, here] = gate
            up_store[:, here] = upper
            hidden[:, here] = (gate * jax.nn.sigmoid(gate) * upper).astype(BF16)

        @pl.loop(0, peers)
        def _(index):
            here = pl.ds(pl.multiple_of(index * part, part), part)
            partial[index] = jnp.dot(
                hidden[...], dmat[:, here], preferred_element_type=F32
            ).astype(BF16)


def sum_kernel(flags, arrived, whole, *refs, stage, axis):
    out = refs[-1]
    part = out.shape[axis]

    @pl.when(flags[0] == stage)
    def _():
        here = pl.ds(pl.multiple_of(flags[1] * part, part), part)
        total = (whole[:, here] if axis else whole[here, :]).astype(F32)
        for index in range(arrived.shape[0]):
            total = total + arrived[index].astype(F32)
        out[...] = total.astype(BF16)


def last_sum_kernel(flags, arrived, xval, cot, out, *, final):
    rows, part = out.shape
    here = pl.ds(pl.multiple_of(flags[1] * part, part), part)
    total = jnp.sum(arrived[...].astype(F32), axis=0)

    @pl.when(flags[0] == final)
    def _():
        out[...] = (total + xval[:, here].astype(F32)).astype(BF16)

    @pl.when(flags[0] != final)
    def _():
        out[...] = (total + cot[here, :].astype(F32).T).astype(BF16)


def last_partial_kernel(flags, last, partial, out, *, final):
    @pl.when(flags[0] == final)
    def _():
        out[...] = last[...]

    @pl.when(flags[0] != final)
    def _():
        @pl.loop(0, out.shape[0])
        def _(index):
            out[index] = partial[index].astype(F32).T.astype(BF16)


def outputs_kernel(flags, end, even_x, odd_x, even_cot, odd_cot, section_out, section_grad, *, final):
    peers, rows, part = end.shape
    odd = lax.rem(flags[0], 2) == 1

    def fill(condition, target, value):
        @pl.when(condition)
        def _():
            @pl.loop(0, peers)
            def _(index):
                here = pl.ds(pl.multiple_of(index * part, part), part)
                target[0, :, here] = value(index, here)

    fill(flags[0] == final, section_out, lambda index, here: end[index].astype(F32))
    fill((flags[0] != final) & odd, section_out, lambda index, here: odd_x[:, here].astype(F32))
    fill(
        (flags[0] != final) & jnp.logical_not(odd),
        section_out,
        lambda index, here: even_x[:, here].astype(F32),
    )
    fill(flags[0] == 0, section_grad, lambda index, here: end[index].astype(F32))
    fill((flags[0] != 0) & odd, section_grad, lambda index, here: even_cot[here, :].astype(F32).T)
    fill(
        (flags[0] != 0) & jnp.logical_not(odd),
        section_grad,
        lambda index, here: odd_cot[here, :].astype(F32).T,
    )


def turn_kernel(xval, gate, upper, xturned, gate_turned, up_turned):
    @pl.loop(0, xval.shape[1] // BLOCK)
    def _(index):
        here = pl.ds(pl.multiple_of(index * BLOCK, BLOCK), BLOCK)
        xturned[here, :] = xval[:, here].astype(F32).T.astype(BF16)

    @pl.loop(0, gate.shape[1] // BLOCK)
    def _(index):
        here = pl.ds(pl.multiple_of(index * BLOCK, BLOCK), BLOCK)
        gate_turned[here, :] = gate[:, here].T
        up_turned[here, :] = upper[:, here].T


def backward_kernel(flags, *refs, peers, stage, count):
    pieces = refs[:count]
    gain, gmat, umat, dmat, xval, gate_store, up_store = refs[count : count + 7]
    cot, partial, dgate, dup = refs[-4:]
    width, cols = gmat.shape
    part, rows = width // peers, xval.shape[1]
    tile = tile_of(cols)

    @pl.when(flags[0] == stage)
    def _():
        def store(place, value):
            cot[pl.ds(place, part), :] = value

        if count == 1:
            pltpu.sync_copy(pieces[0], cot)
        else:
            place_pieces(flags, pieces, peers, part, store)

        def square(index, total):
            here = xval[pl.ds(pl.multiple_of(index * part, part), part), :].astype(F32)
            return total + jnp.sum(here * here, axis=0, keepdims=True)

        total = lax.fori_loop(0, peers, square, jnp.zeros((1, rows), F32))
        scale = lax.rsqrt(total / width + EPS)

        def hidden_side(index, inner):
            here = pl.ds(pl.multiple_of(index * tile, tile), tile)
            dhid = jnp.dot(dmat[here, :], cot[...], preferred_element_type=F32)
            gate = gate_store[here, :]
            upper = up_store[here, :]
            sig = jax.nn.sigmoid(gate)
            dgate_low = (dhid * upper * sig * (1.0 + gate * (1.0 - sig))).astype(BF16)
            dup_low = (dhid * gate * sig).astype(BF16)
            dgate[here, :] = dgate_low
            dup[here, :] = dup_low
            both = dgate_low.astype(F32) * gate + dup_low.astype(F32) * upper
            return inner + jnp.sum(both, axis=0, keepdims=True)

        inner = lax.fori_loop(0, cols // tile, hidden_side, jnp.zeros((1, rows), F32))
        pull = scale * scale * inner / width

        @pl.loop(0, peers)
        def _(index):
            here = pl.ds(pl.multiple_of(index * part, part), part)
            dnorm = jnp.dot(gmat[here, :], dgate[...], preferred_element_type=F32) + jnp.dot(
                umat[here, :], dup[...], preferred_element_type=F32
            )
            back = scale * dnorm * gain[here, :] - xval[here, :].astype(F32) * pull
            partial[index] = back.astype(BF16)


def local(inputs, out_grad, norm_gain, gate_weight, up_weight, down_weight, block_mask):
    stages, peers = lax.axis_size("pipe"), lax.axis_size("tensor")
    stage, peer = lax.axis_index("pipe"), lax.axis_index("tensor")
    rows, part = inputs.shape
    width, cols = gate_weight.shape[1:]
    flags = jnp.stack([stage, peer]).astype(jnp.int32)
    vmem = functools.partial(pltpu.CompilerParams, vmem_limit_bytes=12 * 2**20)
    in_hbm = functools.partial(pltpu.with_memory_space_constraint, memory_space=pltpu.HBM)
    in_vmem = functools.partial(pltpu.with_memory_space_constraint, memory_space=pltpu.VMEM)

    tall_gain = jnp.broadcast_to(norm_gain.reshape(width, 1), (width, rows))
    grad_copies = jnp.broadcast_to(out_grad.T, (peers, part, rows))
    weights = pl.pallas_call(
        load_kernel,
        out_shape=(
            pltpu.VMEM((width, cols), BF16),
            pltpu.VMEM((width, cols), BF16),
            pltpu.VMEM((cols, width), BF16),
        ),
        in_specs=[SMEM_WHOLE] + [HBM_WHOLE] * 3 + [pl.BlockSpec(memory_space=pl.ANY), HBM_WHOLE, SMEM_WHOLE],
        out_specs=(VMEM_WHOLE,) * 3,
        scratch_shapes=[pltpu.SemaphoreType.DMA((3, 4))],
        compiler_params=vmem(),
        cost_estimate=pl.CostEstimate(flops=0, bytes_accessed=6 * width * cols, transcendentals=0),
        name="load_masked",
    )(block_mask.reshape(-1), gate_weight, up_weight, down_weight, tall_gain, in_hbm(grad_copies), flags)
    weights = [in_vmem(weight) for weight in weights]

    cost = pl.CostEstimate(
        flops=6 * rows * width * cols, bytes_accessed=6 * width * cols, transcendentals=0
    )
    small_cost = pl.CostEstimate(flops=0, bytes_accessed=4 * rows * width, transcendentals=0)
    hidden_type = pltpu.VMEM((rows, cols), F32)
    turned_type = pltpu.VMEM((cols, rows), F32)
    wide_type = pltpu.VMEM((rows, width), BF16)
    tall_type = pltpu.VMEM((width, rows), BF16)

    def forward(at, pieces, kept):
        count, held = len(pieces), len(kept)
        return pl.pallas_call(
            functools.partial(forward_kernel, peers=peers, stage=at, count=count),
            out_shape=(wide_type, hidden_type, hidden_type, jax.ShapeDtypeStruct((peers, rows, part), BF16)),
            in_specs=[SMEM_WHOLE] + [VMEM_WHOLE] * (count + 4 + held),
            out_specs=(VMEM_WHOLE,) * 4,
            scratch_shapes=[pltpu.VMEM((rows, width), BF16), pltpu.VMEM((rows, cols), BF16)],
            input_output_aliases={count + 5 + index: index for index in range(held)},
            compiler_params=vmem(),
            cost_estimate=cost,
            name="forward_layer",
        )(flags, *map(in_vmem, pieces), in_vmem(norm_gain), *weights, *map(in_vmem, kept))

    def backward(at, pieces, kept, cot):
        count, held = len(pieces), len(cot)
        return pl.pallas_call(
            functools.partial(backward_kernel, peers=peers, stage=at, count=count),
            out_shape=(tall_type, jax.ShapeDtypeStruct((peers, part, rows), BF16)),
            in_specs=[SMEM_WHOLE]
            + [HBM_WHOLE if count == 1 else VMEM_WHOLE] * count
            + [VMEM_WHOLE] * (7 + held),
            out_specs=(VMEM_WHOLE,) * 2,
            scratch_shapes=[pltpu.VMEM((cols, rows), BF16), pltpu.VMEM((cols, rows), BF16)],
            input_output_aliases={count + 8 + index: index for index in range(held)},
            compiler_params=vmem(),
            cost_estimate=cost,
            name="backward_layer",
        )(
            flags,
            *map(in_hbm if count == 1 else in_vmem, pieces),
            tall_gain,
            *weights,
            *map(in_vmem, kept),
            *map(in_vmem, cot),
        )

    def summed(at, partial, whole, axis, passed=()):
        arrived = lax.all_to_all(partial, "tensor", 0, 0)
        any_spec = HBM_WHOLE
        return pl.pallas_call(
            functools.partial(sum_kernel, stage=at, axis=axis),
            out_shape=[pltpu.HBM(value.shape, value.dtype) for value in passed]
            + [pltpu.VMEM(arrived.shape[1:], BF16)],
            in_specs=[SMEM_WHOLE] + [VMEM_WHOLE] * 2 + [any_spec] * len(passed),
            out_specs=[any_spec] * len(passed) + [VMEM_WHOLE],
            input_output_aliases={3 + index: index for index in range(len(passed))},
            compiler_params=vmem(),
            cost_estimate=small_cost,
            name="sum_pieces",
        )(flags, in_vmem(arrived), in_vmem(whole), *map(in_hbm, passed))

    def turned(kept):
        return pl.pallas_call(
            turn_kernel,
            out_shape=(tall_type, turned_type, turned_type),
            in_specs=[VMEM_WHOLE] * 3,
            out_specs=(VMEM_WHOLE,) * 3,
            compiler_params=vmem(),
            cost_estimate=small_cost,
            name="turn_kept",
        )(*map(in_vmem, kept))

    def moved(value, source, target, step):
        stride = target - source
        pairs = []
        for start in range(source % 2, stages, 2):
            if 0 <= start + stride < stages:
                pairs += [
                    (start * peers + who, (start + stride) * peers + (who + step) % peers)
                    for who in range(peers)
                ]
        return lax.ppermute(value, ("pipe", "tensor"), pairs)

    def spread(value, source, target):
        return [moved(value, source, target, step) for step in range(peers)]

    def gathered(shard):
        return lax.all_to_all(jnp.broadcast_to(shard, (peers,) + shard.shape), "tensor", 0, 0)

    kept, pieces = [], [gathered(inputs)]
    for at in range(stages):
        *kept, partial = forward(at, pieces, kept)
        if at < stages - 1:
            *passed, shard = summed(at, partial, kept[0], 1, () if at else (grad_copies,))
            if at == 0:
                last_pieces = [lax.all_to_all(passed[0], "tensor", 0, 0).reshape(width, rows)]
            pieces = spread(shard, at, at + 1)
    last_partial, xval = partial, kept[0]

    kept, cot, pieces = turned(kept), [], last_pieces
    for at in range(stages - 1, -1, -1):
        *cot, partial = backward(at, pieces, kept, cot)
        if at > 0:
            pieces = spread(summed(at, partial, cot[0], 0)[0], at, at - 1)
    cot = cot[0]

    final = stages - 1
    both = pl.pallas_call(
        functools.partial(last_partial_kernel, final=final),
        out_shape=pltpu.VMEM((peers, rows, part), BF16),
        in_specs=[SMEM_WHOLE] + [VMEM_WHOLE] * 2,
        out_specs=VMEM_WHOLE,
        compiler_params=vmem(),
        cost_estimate=small_cost,
        name="last_partial",
    )(flags, last_partial, in_vmem(partial))
    shard = pl.pallas_call(
        functools.partial(last_sum_kernel, final=final),
        out_shape=pltpu.VMEM((rows, part), BF16),
        in_specs=[SMEM_WHOLE] + [VMEM_WHOLE] * 3,
        out_specs=VMEM_WHOLE,
        compiler_params=vmem(),
        cost_estimate=small_cost,
        name="last_sum",
    )(flags, in_vmem(lax.all_to_all(both, "tensor", 0, 0)), in_vmem(xval), in_vmem(cot))
    end = gathered(shard)
    neighbours = (
        moved(xval, 1, 0, 0),
        moved(xval, 2, 1, 0),
        moved(cot, 0, 1, 0),
        moved(cot, 1, 2, 0),
    )
    return pl.pallas_call(
        functools.partial(outputs_kernel, final=final),
        out_shape=(jax.ShapeDtypeStruct((1, rows, width), F32),) * 2,
        in_specs=[SMEM_WHOLE] + [VMEM_WHOLE] * 5,
        out_specs=(VMEM_WHOLE,) * 2,
        compiler_params=vmem(vmem_limit_bytes=24 * 2**20),
        cost_estimate=small_cost,
        name="write_outputs",
    )(flags, end, *neighbours)


def solution(mesh):
    in_specs = (
        P(None, "tensor"),
        P(None, "tensor"),
        P("pipe", None),
        P("pipe", None, "tensor"),
        P("pipe", None, "tensor"),
        P("pipe", "tensor", None),
        P("pipe", None, None, "tensor"),
    )
    out_specs = (P("pipe", None, None), P("pipe", None, None))
    return jax.shard_map(local, mesh=mesh, in_specs=in_specs, out_specs=out_specs, check_vma=False)
```

time: 603 us -> 593 us (0.983); the launches traced: 601 us -> 584 us
  starting transfers between devices: 294 us -> 111 us
  local copies, waits for them, and re-layouts: 23.4 us -> 117 us
  waiting for transfers between devices: 49.1 us -> 87.3 us
  blocking collectives: 163 us -> 192 us
  Pallas kernels: 60.4 us -> 74.4 us
  other arithmetic: 9.59 us -> 0.65 us
    ppermute x64 -> x52, starting transfers between devices: 290 us -> 95.7 us  [moved(): return lax.ppermute(value, ('pipe', 'tensor'), pairs)]
    unnamed x49 -> x89, local copies, waits for them, and re-layouts: 21.3 us -> 108 us
    ppermute x64 -> x52, waiting for transfers between devices: 32.7 us -> 81.3 us  [moved(): return lax.ppermute(value, ('pipe', 'tensor'), pairs)]
    all_to_all x0 -> x1, blocking collectives: none -> 32 us  [local(): lax.all_to_all(both, 'tensor', 0, 0)]
    pallas_call x8 -> x18, Pallas kernels: 41.2 us -> 55.2 us  [the longest x4 25.1 us: backward(): pl.pallas_call(functools.partial(backward_kernel, peers=peers, stage=at,...]
    all_to_all x1 -> x3, starting transfers between devices: 4.26 us -> 15.8 us  [the longest x2 11.5 us: gathered(): lax.all_to_all(jnp.broadcast_to(shard, (peers,) + shard.shape), 'tensor',...]
    all_to_all x1 -> x3, waiting for transfers between devices: 16.4 us -> 5.96 us  [the longest x2 5.96 us: gathered(): lax.all_to_all(jnp.broadcast_to(shard, (peers,) + shard.shape), 'tensor',...]
    broadcast_in_dim x1 -> x4, local copies, waits for them, and re-layouts: 0.08 us -> 6.82 us  [the longest x2 3.02 us: gathered(): jnp.broadcast_to(shard, (peers,) + shard.shape)]
  transfers between devices with their start and end apart: 65 -> 55, of which waited for: 10 -> 14; matrix products, arithmetic and copies ran while one was open for 1% -> 1% of each run, Pallas kernels for 3% -> 4%
where the time goes in v2:
time: 593 us; the launch traced here: 584 us
  blocking collectives  192 us (32%)
  local copies, waits for them, and re-layouts  117 us (20%)
  starting transfers between devices  111 us (19%)
  waiting for transfers between devices  87.3 us (15%)
  Pallas kernels  74.4 us (13%)
    all_to_all x6, blocking collectives, summed(): arrived = lax.all_to_all(partial, 'tensor', 0, 0)  160 us
    unnamed x89, local copies, waits for them, and re-layouts  108 us
    ppermute x52, starting transfers between devices, moved(): return lax.ppermute(value, ('pipe', 'tensor'), pairs)  95.7 us
    ppermute x52, waiting for transfers between devices, moved(): return lax.ppermute(value, ('pipe', 'tensor'), pairs)  81.3 us
    all_to_all x1, blocking collectives, local(): lax.all_to_all(both, 'tensor', 0, 0)  32 us
    pallas_call x4, Pallas kernels, backward(): pl.pallas_call(functools.partial(backward_kernel, peers=peers, stage=at,...  25.1 us
    pallas_call x1, Pallas kernels, local(): pl.pallas_call(load_kernel, out_shape=(pltpu.VMEM((width, cols), BF16), p...  19.2 us
    pallas_call x4, Pallas kernels, forward(): pl.pallas_call(functools.partial(forward_kernel, peers=peers, stage=at, c...  16.8 us
  transfers between devices with their start and end apart: 55, of which 14 were waited for; matrix products, arithmetic and copies ran while one was open for 1% of the time, Pallas kernels for 4%

profile of v2, /device:TPU:0, one launch (start us, length us, event | category | flops | bytes accessed | tf_op | source)
XLA Modules:
  0.0 584.2 jit_solution(10906156092609890281)
XLA Ops:
  2.6 7.3 %all-to-all-start = ((bf16[8,128,512]{2,1,0:T(8,128)(2,1)}), bf16[8,128,512]{2,1,0:T(8,128)(2,1)S(1)}, u32[]{:S(2)}, u32[]{:S(2)}) async-start(bf16[8,128,512]{2,1,0:T(8,128)(2,1)} %broadcast_in_dim.16), calls=%async_computation | async-start | bytes 2097152 | tf_op jit(solution)/shard_map/all_to_all | solution.py:363
  16.9 19.2 %load_masked.1 = (bf16[4096,1792]{1,0:T(8,128)(2,1)S(1)}, bf16[4096,1792]{1,0:T(8,128)(2,1)S(1)}, bf16[1792,4096]{1,0:T(8,128)(2,1)S(1)}) custom-call(s32[1344]{0:T(1024)} %reshape.12.mask, bf16[1,4096,1792]{2,1,0:T(8,128)(2,1)} %gate_hbm.1, bf16[1,4096,1792]{2,1,0:T(8,128)(2,1)} %up_hbm.1, bf16[1,1792,4096]{2,1,0:T(8,128)(2,1)} %down_hbm.1, ...), custom_call_target="tpu_custom_call" | custom-call | bytes 44040192 | tf_op jit(solution)/shard_map/load_masked/pallas_call | solution.py:260
  41.2 5.2 copy-done.9
  52.5 5.2 copy-done.1
  57.7 5.2 copy-done.10
  62.9 5.2 copy-done.14
  69.3 11.6 %forward_layer.4 = (bf16[128,4096]{1,0:T(8,128)(2,1)S(1)}, f32[128,1792]{1,0:T(8,128)S(1)}, f32[128,1792]{1,0:T(8,128)S(1)}, bf16[8,128,512]{2,1,0:T(8,128)(2,1)}) custom-call(s32[2]{0:T(128)} %pad_add_fusion.refs_2_.flags, bf16[8,128,512]{2,1,0:T(8,128)(2,1)S(1)} %copy-done.24, f32[1,4096]{1,0:T(1,128)S(1)} %copy-done.36, bf16[4096,1792]{1,0:T(8,128)(2,1)S(1)} %copy-done.1, ...), custom_call_target="tpu_custom_call" | custom-call | flops 5637144576 | bytes 44040192 | tf_op jit(solution)/shard_map/forward_layer/pallas_call | solution.py:287
  80.9 22.0 %all_to_all.50.arrived = bf16[8,128,512]{2,1,0:T(8,128)(2,1)S(1)} all-to-all(bf16[8,128,512]{2,1,0:T(8,128)(2,1)} %get-tuple-element.37), channel_id=1, replica_groups=mesh['pipe'=4,'tensor'=8] {'tensor'}, dimensions={0} | all-to-all | bytes 2097152 | tf_op jit(solution)/shard_map/all_to_all | solution.py:323
  117.0 5.2 copy-done.2
  124.0 21.3 %all_to_all.51.arrived = bf16[8,128,512]{2,1,0:T(8,128)(2,1)S(1)} all-to-all(bf16[8,128,512]{2,1,0:T(8,128)(2,1)} %get-tuple-element.42), channel_id=1, replica_groups=mesh['pipe'=4,'tensor'=8] {'tensor'}, dimensions={0} | all-to-all | bytes 2097152 | tf_op jit(solution)/shard_map/all_to_all | solution.py:323
  158.3 30.0 %all_to_all.52.arrived = bf16[8,128,512]{2,1,0:T(8,128)(2,1)} all-to-all(bf16[8,128,512]{2,1,0:T(8,128)(2,1)} %get-tuple-element.46), channel_id=1, replica_groups=mesh['pipe'=4,'tensor'=8] {'tensor'}, dimensions={0} | all-to-all | bytes 2097152 | tf_op jit(solution)/shard_map/all_to_all | solution.py:323
  194.4 33.6 %collective-permute-start.16 = (bf16[128,512]{1,0:T(8,128)(2,1)S(1)}, bf16[128,512]{1,0:T(8,128)(2,1)S(1)}, u32[]{:S(2)}, u32[]{:S(2)}) collective-permute-start(bf16[128,512]{1,0:T(8,128)(2,1)S(1)} %sum_pieces.8), channel_id=1, source_target_pairs={{0,8},{1,9},{2,10},{3,11},{4,12},{5,13},{6,14},{7,15},{16,24},{17,... | collective-permute-start | bytes 393224 | tf_op jit(solution)/shard_map/ppermute | solution.py:357
  243.9 5.2 copy-done.4
  249.1 5.2 copy-done.11
  269.7 5.2 copy-done.5
  290.2 38.0 %all_to_all.53.arrived = bf16[8,512,128]{2,1,0:T(8,128)(2,1)S(1)} all-to-all(bf16[8,512,128]{2,1,0:T(8,128)(2,1)} %get-tuple-element.58), channel_id=1, replica_groups=mesh['pipe'=4,'tensor'=8] {'tensor'}, dimensions={0} | all-to-all | bytes 2097152 | tf_op jit(solution)/shard_map/all_to_all | solution.py:323
  347.9 5.2 copy-done.6
  355.6 29.0 %all_to_all.54.arrived = bf16[8,512,128]{2,1,0:T(8,128)(2,1)S(1)} all-to-all(bf16[8,512,128]{2,1,0:T(8,128)(2,1)} %get-tuple-element.60), channel_id=1, replica_groups=mesh['pipe'=4,'tensor'=8] {'tensor'}, dimensions={0} | all-to-all | bytes 2097152 | tf_op jit(solution)/shard_map/all_to_all | solution.py:323
  398.4 19.5 %all_to_all.55.arrived = bf16[8,512,128]{2,1,0:T(8,128)(2,1)S(1)} all-to-all(bf16[8,512,128]{2,1,0:T(8,128)(2,1)} %get-tuple-element.62), channel_id=1, replica_groups=mesh['pipe'=4,'tensor'=8] {'tensor'}, dimensions={0} | all-to-all | bytes 2097152 | tf_op jit(solution)/shard_map/all_to_all | solution.py:323
  425.0 57.9 %collective-permute-done.40.refs_0_ = bf16[512,128]{1,0:T(8,128)(2,1)S(1)} collective-permute-done((bf16[512,128]{1,0:T(8,128)(2,1)S(1)}, bf16[512,128]{1,0:T(8,128)(2,1)S(1)}, u32[]{:S(2)}, u32[]{:S(2)}) %collective-permute-start.40) | collective-permute-done | bytes 131104 | tf_op jit(solution)/shard_map/ppermute | solution.py:357
  496.6 5.2 copy-done.8
  501.8 17.4 %backward_layer.7 = (bf16[4096,128]{1,0:T(8,128)(2,1)S(1)}, bf16[8,512,128]{2,1,0:T(8,128)(2,1)}) custom-call(s32[2]{0:T(128)} %pad_add_fusion.refs_2_.flags, bf16[512,128]{1,0:T(8,128)(2,1)S(1)} %collective-permute-done.40.refs_0_, bf16[512,128]{1,0:T(8,128)(2,1)S(1)} %collective-permute-done.41.refs_1_, ...), custom_call_target="tpu_custom_call", output_to_operand_aliasing={{0}: (16, {})} | custom-call | flops 5637144576 | bytes 44040192 | tf_op jit(solution)/shard_map/backward_layer/pallas_call | solution.py:301
  521.8 32.0 %all_to_all.56.arrived = bf16[8,128,512]{2,1,0:T(8,128)(2,1)S(1)} all-to-all(bf16[8,128,512]{2,1,0:T(8,128)(2,1)S(1)} %last_partial.1), channel_id=1, replica_groups=mesh['pipe'=4,'tensor'=8] {'tensor'}, dimensions={0} | all-to-all | bytes 2097152 | tf_op jit(solution)/shard_map/all_to_all | solution.py:400
  570.5 6.0 %all-to-all-done.9.end = bf16[8,128,512]{2,1,0:T(8,128)(2,1)S(1)} async-done(((bf16[8,128,512]{2,1,0:T(8,128)(2,1)}), bf16[8,128,512]{2,1,0:T(8,128)(2,1)S(1)}, u32[]{:S(2)}, u32[]{:S(2)}) %all-to-all-start.9) | async-done | bytes 1048608 | tf_op jit(solution)/shard_map/all_to_all | solution.py:363
  (208 shorter events, 186.2 us)
Async XLA Ops:
  2.6 49.0 %all-to-all-start = ((bf16[8,128,512]{2,1,0:T(8,128)(2,1)}), bf16[8,128,512]{2,1,0:T(8,128)(2,1)S(1)}, u32[]{:S(2)}, u32[]{:S(2)}) async-start(bf16[8,128,512]{2,1,0:T(8,128)(2,1)} %broadcast_in_dim.16), calls=%async_computation | async-start | bytes 2097152 | tf_op jit(solution)/shard_map/all_to_all | solution.py:363
  107.5 7.0 %collective-permute-start.3 = (bf16[128,512]{1,0:T(8,128)(2,1)S(1)}, bf16[128,512]{1,0:T(8,128)(2,1)S(1)}, u32[]{:S(2)}, u32[]{:S(2)}) collective-permute-start(bf16[128,512]{1,0:T(8,128)(2,1)S(1)} %get-tuple-element.39), channel_id=1, source_target_pairs={{0,11},{1,12},{2,13},{3,14},{4,15},{5,8},{6,9},{7,10},{16,27},{17,... | collective-permute-start | bytes 393224 | tf_op jit(solution)/shard_map/ppermute | solution.py:357
  188.4 81.4 %all-to-all-start.4 = ((bf16[8,512,128]{2,1,0:T(8,128)(2,1)}), bf16[8,512,128]{2,1,0:T(8,128)(2,1)}, u32[]{:S(2)}, u32[]{:S(2)}) async-start(bf16[8,512,128]{2,1,0:T(8,128)(2,1)} %get-tuple-element.51), calls=%async_computation.4 | async-start | bytes 2097152 | tf_op jit(solution)/shard_map/all_to_all | solution.py:371
  194.4 40.9 %collective-permute-start.16 = (bf16[128,512]{1,0:T(8,128)(2,1)S(1)}, bf16[128,512]{1,0:T(8,128)(2,1)S(1)}, u32[]{:S(2)}, u32[]{:S(2)}) collective-permute-start(bf16[128,512]{1,0:T(8,128)(2,1)S(1)} %sum_pieces.8), channel_id=1, source_target_pairs={{0,8},{1,9},{2,10},{3,11},{4,12},{5,13},{6,14},{7,15},{16,24},{17,... | collective-permute-start | bytes 393224 | tf_op jit(solution)/shard_map/ppermute | solution.py:357
  228.0 9.5 %collective-permute-start.17 = (bf16[128,512]{1,0:T(8,128)(2,1)S(1)}, bf16[128,512]{1,0:T(8,128)(2,1)S(1)}, u32[]{:S(2)}, u32[]{:S(2)}) collective-permute-start(bf16[128,512]{1,0:T(8,128)(2,1)S(1)} %sum_pieces.8), channel_id=1, source_target_pairs={{0,9},{1,10},{2,11},{3,12},{4,13},{5,14},{6,15},{7,8},{16,25},{17,... | collective-permute-start | bytes 393224 | tf_op jit(solution)/shard_map/ppermute | solution.py:357
  230.5 9.5 %collective-permute-start.18 = (bf16[128,512]{1,0:T(8,128)(2,1)S(1)}, bf16[128,512]{1,0:T(8,128)(2,1)S(1)}, u32[]{:S(2)}, u32[]{:S(2)}) collective-permute-start(bf16[128,512]{1,0:T(8,128)(2,1)S(1)} %sum_pieces.8), channel_id=1, source_target_pairs={{0,10},{1,11},{2,12},{3,13},{4,14},{5,15},{6,8},{7,9},{16,26},{17,... | collective-permute-start | bytes 393224 | tf_op jit(solution)/shard_map/ppermute | solution.py:357
  231.8 9.6 %collective-permute-start.19 = (bf16[128,512]{1,0:T(8,128)(2,1)S(1)}, bf16[128,512]{1,0:T(8,128)(2,1)S(1)}, u32[]{:S(2)}, u32[]{:S(2)}) collective-permute-start(bf16[128,512]{1,0:T(8,128)(2,1)S(1)} %sum_pieces.8), channel_id=1, source_target_pairs={{0,11},{1,12},{2,13},{3,14},{4,15},{5,8},{6,9},{7,10},{16,27},{17,... | collective-permute-start | bytes 393224 | tf_op jit(solution)/shard_map/ppermute | solution.py:357
  234.0 7.4 %collective-permute-start.20 = (bf16[128,512]{1,0:T(8,128)(2,1)S(1)}, bf16[128,512]{1,0:T(8,128)(2,1)S(1)}, u32[]{:S(2)}, u32[]{:S(2)}) collective-permute-start(bf16[128,512]{1,0:T(8,128)(2,1)S(1)} %sum_pieces.8), channel_id=1, source_target_pairs={{0,12},{1,13},{2,14},{3,15},{4,8},{5,9},{6,10},{7,11},{16,28},{17,... | collective-permute-start | bytes 393224 | tf_op jit(solution)/shard_map/ppermute | solution.py:357
  330.0 9.0 %collective-permute-start.25 = (bf16[512,128]{1,0:T(8,128)(2,1)S(1)}, bf16[512,128]{1,0:T(8,128)(2,1)S(1)}, u32[]{:S(2)}, u32[]{:S(2)}) collective-permute-start(bf16[512,128]{1,0:T(8,128)(2,1)S(1)} %sum_pieces.9), channel_id=1, source_target_pairs={{8,1},{9,2},{10,3},{11,4},{12,5},{13,6},{14,7},{15,0},{24,17},{25,... | collective-permute-start | bytes 393224 | tf_op jit(solution)/shard_map/ppermute | solution.py:357
  331.3 9.0 %collective-permute-start.26 = (bf16[512,128]{1,0:T(8,128)(2,1)S(1)}, bf16[512,128]{1,0:T(8,128)(2,1)S(1)}, u32[]{:S(2)}, u32[]{:S(2)}) collective-permute-start(bf16[512,128]{1,0:T(8,128)(2,1)S(1)} %sum_pieces.9), channel_id=1, source_target_pairs={{8,2},{9,3},{10,4},{11,5},{12,6},{13,7},{14,0},{15,1},{24,18},{25,... | collective-permute-start | bytes 393224 | tf_op jit(solution)/shard_map/ppermute | solution.py:357
  332.6 12.1 %collective-permute-start.27 = (bf16[512,128]{1,0:T(8,128)(2,1)S(1)}, bf16[512,128]{1,0:T(8,128)(2,1)S(1)}, u32[]{:S(2)}, u32[]{:S(2)}) collective-permute-start(bf16[512,128]{1,0:T(8,128)(2,1)S(1)} %sum_pieces.9), channel_id=1, source_target_pairs={{8,3},{9,4},{10,5},{11,6},{12,7},{13,0},{14,1},{15,2},{24,19},{25,... | collective-permute-start | bytes 393224 | tf_op jit(solution)/shard_map/ppermute | solution.py:357
  333.9 11.9 %collective-permute-start.28 = (bf16[512,128]{1,0:T(8,128)(2,1)S(1)}, bf16[512,128]{1,0:T(8,128)(2,1)S(1)}, u32[]{:S(2)}, u32[]{:S(2)}) collective-permute-start(bf16[512,128]{1,0:T(8,128)(2,1)S(1)} %sum_pieces.9), channel_id=1, source_target_pairs={{8,4},{9,5},{10,6},{11,7},{12,0},{13,1},{14,2},{15,3},{24,20},{25,... | collective-permute-start | bytes 393224 | tf_op jit(solution)/shard_map/ppermute | solution.py:357
  335.2 10.6 %collective-permute-start.29 = (bf16[512,128]{1,0:T(8,128)(2,1)S(1)}, bf16[512,128]{1,0:T(8,128)(2,1)S(1)}, u32[]{:S(2)}, u32[]{:S(2)}) collective-permute-start(bf16[512,128]{1,0:T(8,128)(2,1)S(1)} %sum_pieces.9), channel_id=1, source_target_pairs={{8,5},{9,6},{10,7},{11,0},{12,1},{13,2},{14,3},{15,4},{24,21},{25,... | collective-permute-start | bytes 393224 | tf_op jit(solution)/shard_map/ppermute | solution.py:357
  339.0 8.8 %collective-permute-start.30 = (bf16[512,128]{1,0:T(8,128)(2,1)S(1)}, bf16[512,128]{1,0:T(8,128)(2,1)S(1)}, u32[]{:S(2)}, u32[]{:S(2)}) collective-permute-start(bf16[512,128]{1,0:T(8,128)(2,1)S(1)} %sum_pieces.9), channel_id=1, source_target_pairs={{8,6},{9,7},{10,0},{11,1},{12,2},{13,3},{14,4},{15,5},{24,22},{25,... | collective-permute-start | bytes 393224 | tf_op jit(solution)/shard_map/ppermute | solution.py:357
  340.3 7.6 %collective-permute-start.31 = (bf16[512,128]{1,0:T(8,128)(2,1)S(1)}, bf16[512,128]{1,0:T(8,128)(2,1)S(1)}, u32[]{:S(2)}, u32[]{:S(2)}) collective-permute-start(bf16[512,128]{1,0:T(8,128)(2,1)S(1)} %sum_pieces.9), channel_id=1, source_target_pairs={{8,7},{9,0},{10,1},{11,2},{12,3},{13,4},{14,5},{15,6},{24,23},{25,... | collective-permute-start | bytes 393224 | tf_op jit(solution)/shard_map/ppermute | solution.py:357
  418.5 64.4 %collective-permute-start.40 = (bf16[512,128]{1,0:T(8,128)(2,1)S(1)}, bf16[512,128]{1,0:T(8,128)(2,1)S(1)}, u32[]{:S(2)}, u32[]{:S(2)}) collective-permute-start(bf16[512,128]{1,0:T(8,128)(2,1)S(1)} %sum_pieces.11), channel_id=1, source_target_pairs={{8,0},{9,1},{10,2},{11,3},{12,4},{13,5},{14,6},{15,7},{24,16},{25,... | collective-permute-start | bytes 393224 | tf_op jit(solution)/shard_map/ppermute | solution.py:357
  419.8 68.2 %collective-permute-start.41 = (bf16[512,128]{1,0:T(8,128)(2,1)S(1)}, bf16[512,128]{1,0:T(8,128)(2,1)S(1)}, u32[]{:S(2)}, u32[]{:S(2)}) collective-permute-start(bf16[512,128]{1,0:T(8,128)(2,1)S(1)} %sum_pieces.11), channel_id=1, source_target_pairs={{8,1},{9,2},{10,3},{11,4},{12,5},{13,6},{14,7},{15,0},{24,17},{25,... | collective-permute-start | bytes 393224 | tf_op jit(solution)/shard_map/ppermute | solution.py:357
  421.1 68.1 %collective-permute-start.42 = (bf16[512,128]{1,0:T(8,128)(2,1)S(1)}, bf16[512,128]{1,0:T(8,128)(2,1)S(1)}, u32[]{:S(2)}, u32[]{:S(2)}) collective-permute-start(bf16[512,128]{1,0:T(8,128)(2,1)S(1)} %sum_pieces.11), channel_id=1, source_target_pairs={{8,2},{9,3},{10,4},{11,5},{12,6},{13,7},{14,0},{15,1},{24,18},{25,... | collective-permute-start | bytes 393224 | tf_op jit(solution)/shard_map/ppermute | solution.py:357
  422.4 71.2 %collective-permute-start.43 = (bf16[512,128]{1,0:T(8,128)(2,1)S(1)}, bf16[512,128]{1,0:T(8,128)(2,1)S(1)}, u32[]{:S(2)}, u32[]{:S(2)}) collective-permute-start(bf16[512,128]{1,0:T(8,128)(2,1)S(1)} %sum_pieces.11), channel_id=1, source_target_pairs={{8,3},{9,4},{10,5},{11,6},{12,7},{13,0},{14,1},{15,2},{24,19},{25,... | collective-permute-start | bytes 393224 | tf_op jit(solution)/shard_map/ppermute | solution.py:357
  423.7 70.2 %collective-permute-start.44 = (bf16[512,128]{1,0:T(8,128)(2,1)S(1)}, bf16[512,128]{1,0:T(8,128)(2,1)S(1)}, u32[]{:S(2)}, u32[]{:S(2)}) collective-permute-start(bf16[512,128]{1,0:T(8,128)(2,1)S(1)} %sum_pieces.11), channel_id=1, source_target_pairs={{8,4},{9,5},{10,6},{11,7},{12,0},{13,1},{14,2},{15,3},{24,20},{25,... | collective-permute-start | bytes 393224 | tf_op jit(solution)/shard_map/ppermute | solution.py:357
  482.9 11.0 %collective-permute-start.45 = (bf16[512,128]{1,0:T(8,128)(2,1)S(1)}, bf16[512,128]{1,0:T(8,128)(2,1)S(1)}, u32[]{:S(2)}, u32[]{:S(2)}) collective-permute-start(bf16[512,128]{1,0:T(8,128)(2,1)S(1)} %sum_pieces.11), channel_id=1, source_target_pairs={{8,5},{9,6},{10,7},{11,0},{12,1},{13,2},{14,3},{15,4},{24,21},{25,... | collective-permute-start | bytes 393224 | tf_op jit(solution)/shard_map/ppermute | solution.py:357
  488.0 8.7 %collective-permute-start.46 = (bf16[512,128]{1,0:T(8,128)(2,1)S(1)}, bf16[512,128]{1,0:T(8,128)(2,1)S(1)}, u32[]{:S(2)}, u32[]{:S(2)}) collective-permute-start(bf16[512,128]{1,0:T(8,128)(2,1)S(1)} %sum_pieces.11), channel_id=1, source_target_pairs={{8,6},{9,7},{10,0},{11,1},{12,2},{13,3},{14,4},{15,5},{24,22},{25,... | collective-permute-start | bytes 393224 | tf_op jit(solution)/shard_map/ppermute | solution.py:357
  489.3 7.4 %collective-permute-start.47 = (bf16[512,128]{1,0:T(8,128)(2,1)S(1)}, bf16[512,128]{1,0:T(8,128)(2,1)S(1)}, u32[]{:S(2)}, u32[]{:S(2)}) collective-permute-start(bf16[512,128]{1,0:T(8,128)(2,1)S(1)} %sum_pieces.11), channel_id=1, source_target_pairs={{8,7},{9,0},{10,1},{11,2},{12,3},{13,4},{14,5},{15,6},{24,23},{25,... | collective-permute-start | bytes 393224 | tf_op jit(solution)/shard_map/ppermute | solution.py:357
  555.7 20.7 %all-to-all-start.9 = ((bf16[8,128,512]{2,1,0:T(8,128)(2,1)}), bf16[8,128,512]{2,1,0:T(8,128)(2,1)S(1)}, u32[]{:S(2)}, u32[]{:S(2)}) async-start(bf16[8,128,512]{2,1,0:T(8,128)(2,1)} %broadcast_in_dim.20), calls=%async_computation.9 | async-start | bytes 2097152 | tf_op jit(solution)/shard_map/all_to_all | solution.py:363
  (75 other events, 692.4 us)
